TPU v7x, 32 devices: a whole 2x2x4 slice. The times are simulated.
32 devices in a mesh: groups: 2 (over y), owner: 4 (over z), head: 4 (over x, core).
Axes of the slice: x: 2, y: 2, z: 4, core: 2. Of those that a mesh axis runs over, the one named last changes fastest.
Arguments:
- tokens: bfloat16 [16384, 1024], P(('groups', 'owner')), parts along dimension 0, may hold values from -12 to 12
- d_out: bfloat16 [16384, 1024], P(('groups', 'owner')), parts along dimension 0, may hold values from -6 to 6
- w_query: bfloat16 [1024, 1024], P(None, 'head'), may hold values from -0.25 to 0.25
- w_key: bfloat16 [1024, 1024], P(None, 'head'), may hold values from -0.25 to 0.25
- w_value: bfloat16 [1024, 1024], P(None, 'head'), may hold values from -0.25 to 0.25
- w_out: bfloat16 [1024, 1024], P('head'), may hold values from -0.1875 to 0.1875
- fetch_list: int32 [8, 4, 4], P(('groups', 'owner')), parts along dimension 0, may hold values from 0 to 15
- fetch_count: int32 [8, 4], P(('groups', 'owner')), parts along dimension 0, may hold values from 0 to 4
- pattern: int32 [128, 8], P(('groups', 'owner')), parts along dimension 0, may hold values from 0 to 31, as said below
Outputs:
- d_tokens: bfloat16 [16384, 1024], P(('groups', 'owner'), 'head'), parts along dimension 0
- grad_query: float32 [2048, 1024], P(('groups', 'owner'), 'head'), parts along dimension 0
- grad_key: float32 [2048, 1024], P(('groups', 'owner'), 'head'), parts along dimension 0
- grad_value: float32 [2048, 1024], P(('groups', 'owner'), 'head'), parts along dimension 0
- grad_out: float32 [2048, 1024], P(('groups', 'head'), 'owner'), parts along dimension 0
There are 2 independent parts, one for each index of `groups`. A program takes and returns all parts, laid end to end along the dimension named above; an argument that names none is the same for every part. Nothing has to cross between parts.
Inputs may be any that keep to these rules, and one draw needn't show every extreme that they name: `pattern`: column 0 of every row names an owner's own block (below 16).
All inputs are finite; a program needn't handle non-finite values.
Results may differ from a plain program's by a relative error of at most 0.018.
The roundings to bfloat16 on the way count: a program that leaves them out, or rounds other values in their place, can miss the bound.
Values may be sent and summed in bfloat16 or wider, within the bound.
A program may use at most 192 MiB of HBM per device.

v0:
```python
import math

import jax
import jax.numpy as jnp
from jax import lax
from jax.sharding import PartitionSpec as P

HEAD_DIM = 64
BLOCK = 128


def softmax_back(query_grp, grad_grp, key_rows, value_rows, alive):
    scale = 1.0 / math.sqrt(HEAD_DIM)
    scores = (
        jnp.einsum("hgtd,hgsd->hgts", query_grp, key_rows, preferred_element_type=jnp.float32)
        * scale
    )
    scores = jnp.where(alive[None, :, None, :], scores, -1e30)
    probs = jnp.exp(scores - jnp.max(scores, axis=-1, keepdims=True))
    probs = probs / jnp.sum(probs, axis=-1, keepdims=True)
    probs_low = probs.astype(jnp.bfloat16)
    attended = jnp.einsum(
        "hgts,hgsd->hgtd", probs_low, value_rows, preferred_element_type=jnp.float32
    ).astype(jnp.bfloat16)
    row_dot = jnp.sum(grad_grp.astype(jnp.float32) * attended.astype(jnp.float32), axis=-1)
    grad_probs = jnp.einsum(
        "hgtd,hgsd->hgts", grad_grp, value_rows, preferred_element_type=jnp.float32
    )
    grad_scores = (probs * (grad_probs - row_dot[..., None])).astype(jnp.bfloat16)
    grad_q = (
        jnp.einsum("hgts,hgsd->hgtd", grad_scores, key_rows, preferred_element_type=jnp.float32)
        * scale
    )
    grad_k = (
        jnp.einsum("hgts,hgtd->hgsd", grad_scores, query_grp, preferred_element_type=jnp.float32)
        * scale
    )
    grad_v = jnp.einsum("hgts,hgtd->hgsd", probs_low, grad_grp, preferred_element_type=jnp.float32)
    return (attended, grad_q, grad_k, grad_v)


def split_sum(onehot, terms):
    upper = terms.astype(jnp.bfloat16)
    lower = (terms - upper.astype(jnp.float32)).astype(jnp.bfloat16)
    return jnp.einsum(
        "ek,hkbd->hebd", onehot, upper, preferred_element_type=jnp.float32
    ) + jnp.einsum("ek,hkbd->hebd", onehot, lower, preferred_element_type=jnp.float32)


def on_device(tokens, d_out, w_query, w_key, w_value, w_out, fetch_list, fetch_count, pattern):
    owners = lax.axis_size("owner")
    blk_dev, kmax = pattern.shape
    cap = fetch_list.shape[2]
    width = w_query.shape[1]
    heads = width // HEAD_DIM
    rows = tokens.shape[0]
    across = (((1,), (1,)), ((), ()))
    down = (((0,), (0,)), ((), ()))
    query = jnp.dot(tokens, w_query, preferred_element_type=jnp.float32).astype(jnp.bfloat16)
    keys_own = jnp.dot(tokens, w_key, preferred_element_type=jnp.float32).astype(jnp.bfloat16)
    values_own = jnp.dot(tokens, w_value, preferred_element_type=jnp.float32).astype(jnp.bfloat16)
    grad_attn = lax.dot_general(d_out, w_out, across, preferred_element_type=jnp.float32).astype(
        jnp.bfloat16
    )
    key_blocks = keys_own.reshape(blk_dev, BLOCK, heads, HEAD_DIM).transpose(2, 0, 1, 3)
    value_blocks = values_own.reshape(blk_dev, BLOCK, heads, HEAD_DIM).transpose(2, 0, 1, 3)
    requests = fetch_list[0]
    wanted = lax.all_to_all(requests, "owner", split_axis=0, concat_axis=0, tiled=True)
    slot_total = owners * cap
    picked = wanted.reshape(-1)
    fetched_k, fetched_v = (
        lax.all_to_all(key_blocks[:, picked], "owner", split_axis=1, concat_axis=1, tiled=True),
        lax.all_to_all(value_blocks[:, picked], "owner", split_axis=1, concat_axis=1, tiled=True),
    )
    key_ws = jnp.concatenate([key_blocks, fetched_k], axis=1)
    value_ws = jnp.concatenate([value_blocks, fetched_v], axis=1)
    live_slots = (jnp.arange(cap, dtype=jnp.int32)[None, :] < fetch_count[0][:, None]).reshape(-1)
    alive_ws = jnp.concatenate([jnp.ones((blk_dev,), bool), live_slots])
    wset = blk_dev + slot_total
    group = math.gcd(4, blk_dev)
    turns = blk_dev // group
    query_groups = query.reshape(turns, group, BLOCK, heads, HEAD_DIM).transpose(0, 3, 1, 2, 4)
    grad_groups = grad_attn.reshape(turns, group, BLOCK, heads, HEAD_DIM).transpose(0, 3, 1, 2, 4)
    pattern_groups = pattern.reshape(turns, group, kmax)

    def one_step(carry, inputs):
        acc_k, acc_v = carry
        query_grp, grad_grp, entries = inputs
        flat = entries.reshape(-1)
        key_rows = key_ws[:, flat].reshape(heads, group, kmax * BLOCK, HEAD_DIM)
        value_rows = value_ws[:, flat].reshape(heads, group, kmax * BLOCK, HEAD_DIM)
        alive = jnp.repeat(alive_ws[flat].reshape(group, kmax), BLOCK, axis=1)
        attended, grad_q, grad_k, grad_v = softmax_back(
            query_grp, grad_grp, key_rows, value_rows, alive
        )
        onehot = (jnp.arange(wset, dtype=jnp.int32)[:, None] == flat[None, :]).astype(jnp.bfloat16)
        acc_k = acc_k + split_sum(onehot, grad_k.reshape(heads, group * kmax, BLOCK, HEAD_DIM))
        acc_v = acc_v + split_sum(onehot, grad_v.reshape(heads, group * kmax, BLOCK, HEAD_DIM))
        return ((acc_k, acc_v), (attended, grad_q.astype(jnp.bfloat16)))

    start_acc = (
        jnp.zeros((heads, wset, BLOCK, HEAD_DIM), jnp.float32),
        jnp.zeros((heads, wset, BLOCK, HEAD_DIM), jnp.float32),
    )
    (acc_k, acc_v), (attended, grad_q) = lax.scan(
        one_step, start_acc, (query_groups, grad_groups, pattern_groups)
    )
    attended = attended.transpose(0, 2, 3, 1, 4).reshape(rows, width)
    grad_q = grad_q.transpose(0, 2, 3, 1, 4).reshape(rows, width)
    back_k, back_v = (
        lax.all_to_all(
            acc_k[:, blk_dev:].astype(jnp.bfloat16),
            "owner",
            split_axis=1,
            concat_axis=1,
            tiled=True,
        ),
        lax.all_to_all(
            acc_v[:, blk_dev:].astype(jnp.bfloat16),
            "owner",
            split_axis=1,
            concat_axis=1,
            tiled=True,
        ),
    )
    owned = (jnp.arange(blk_dev, dtype=jnp.int32)[:, None] == wanted.reshape(-1)[None, :]).astype(
        jnp.bfloat16
    )
    total_k = acc_k[:, :blk_dev] + jnp.einsum(
        "ek,hkbd->hebd", owned, back_k, preferred_element_type=jnp.float32
    )
    total_v = acc_v[:, :blk_dev] + jnp.einsum(
        "ek,hkbd->hebd", owned, back_v, preferred_element_type=jnp.float32
    )
    grad_k = total_k.astype(jnp.bfloat16).transpose(1, 2, 0, 3).reshape(rows, width)
    grad_v = total_v.astype(jnp.bfloat16).transpose(1, 2, 0, 3).reshape(rows, width)
    term_q = lax.dot_general(tokens, grad_q, down, preferred_element_type=jnp.float32)
    term_k = lax.dot_general(tokens, grad_k, down, preferred_element_type=jnp.float32)
    term_v = lax.dot_general(tokens, grad_v, down, preferred_element_type=jnp.float32)
    term_o = lax.dot_general(attended, d_out, down, preferred_element_type=jnp.float32)
    grad_query, grad_key, grad_value, grad_out = (
        lax.psum_scatter(term_q, "owner", scatter_dimension=0, tiled=True),
        lax.psum_scatter(term_k, "owner", scatter_dimension=0, tiled=True),
        lax.psum_scatter(term_v, "owner", scatter_dimension=0, tiled=True),
        lax.psum_scatter(term_o, "owner", scatter_dimension=1, tiled=True),
    )
    term_x = (
        lax.dot_general(grad_q, w_query, across, preferred_element_type=jnp.float32)
        + lax.dot_general(grad_k, w_key, across, preferred_element_type=jnp.float32)
        + lax.dot_general(grad_v, w_value, across, preferred_element_type=jnp.float32)
    )
    d_tokens = lax.psum_scatter(term_x, "head", scatter_dimension=1, tiled=True).astype(
        jnp.bfloat16
    )
    return (d_tokens, grad_query, grad_key, grad_value, grad_out)


def solution(mesh):
    placed = (
        P(("groups", "owner"), None),
        P(("groups", "owner"), None),
        P(None, "head"),
        P(None, "head"),
        P(None, "head"),
        P("head", None),
        P(("groups", "owner"), None, None),
        P(("groups", "owner"), None),
        P(("groups", "owner"), None),
    )
    return jax.shard_map(
        on_device,
        mesh=mesh,
        in_specs=placed,
        out_specs=(
            P(("groups", "owner"), "head"),
            P(("groups", "owner"), "head"),
            P(("groups", "owner"), "head"),
            P(("groups", "owner"), "head"),
            P(("groups", "head"), "owner"),
        ),
        check_vma=False,
    )
```

profile of v0, /device:TPU:0, one launch (start us, length us, event | category | flops | bytes accessed | tf_op | source)
XLA Modules:
  0.0 671.8 jit_solution(7768452551637539413)
XLA Ops:
  7.2 6.5 all-to-all-start
  28.0 5.1 all-to-all-start.2
  48.9 9.5 %all-to-all-done.2 = bf16[4,16,128,64]{2,3,0,1:T(8,128)(2,1)} async-done(((bf16[4,16,128,64]{2,3,0,1:T(8,128)(2,1)}), bf16[4,16,128,64]{2,3,0,1:T(8,128)(2,1)}, u32[]{:S(2)}, u32[]{:S(2)}) %all-to-all-start.2) | async-done | bytes 1048608 | tf_op jit(solution)/shard_map/all_to_all | solution.py:73
  93.0 342.5 %while.17 = (s32[]{:T(128)}, f32[4,32,128,64]{2,1,3,0:T(8,128)}, f32[4,32,128,64]{2,1,3,0:T(8,128)}, bf16[4,4,4,128,64]{3,4,2,1,0:T(8,128)(2,1)}, bf16[4,4,4,128...) while((s32[]{:T(128)}, f32[4,32,128,64]{2,1,3,0:T(8,128)}, ...), condition=%wide.region_4.5_spmd.clone, body=%wide.region_0.4_spmd.clone.sunk | while | flops 1918767232 | bytes 297073184 | solution.py:105
  95.4 5.2 gather_fusion.2
  107.6 5.2 gather_fusion.1
  119.6 8.8 %fusion.136 = (f32[4,4,128]{2,1,0:T(4,128)S(1)}, f32[4,4,128,1024]{3,2,1,0:T(8,128)}) fusion(pred[4,1024]{1,0:T(4,128)(4,1)S(1)} %bitcast.204, bf16[4,4,1024,64]{2,1,3,0:T(4,128)(2,1)} %reshape.233, bf16[1,4,4,128,64]{3,2,0,4,1:T(4,128)(2,1)S(1)} %get-tuple-element.244), kind=kOutput, calls=%fused_computation.96.clone.1 | convolution fusion | flops 276825088 | bytes 10760192 | tf_op jit(solution)/shard_map/while/body/eval_jaxpr/sub | solution.py:19
  139.6 5.5 reshape.236
  145.1 5.0 multiply_convert_fusion.2
  157.7 5.5 reshape.235
  180.9 5.2 gather_fusion.2
  193.1 5.2 gather_fusion.1
  205.1 8.8 %fusion.136 = (f32[4,4,128]{2,1,0:T(4,128)S(1)}, f32[4,4,128,1024]{3,2,1,0:T(8,128)}) fusion(pred[4,1024]{1,0:T(4,128)(4,1)S(1)} %bitcast.204, bf16[4,4,1024,64]{2,1,3,0:T(4,128)(2,1)} %reshape.233, bf16[1,4,4,128,64]{3,2,0,4,1:T(4,128)(2,1)S(1)} %get-tuple-element.244), kind=kOutput, calls=%fused_computation.96.clone.1 | convolution fusion | flops 276825088 | bytes 10760192 | tf_op jit(solution)/shard_map/while/body/eval_jaxpr/sub | solution.py:19
  225.1 5.5 reshape.236
  243.2 5.5 reshape.235
  266.4 5.2 gather_fusion.2
  278.6 5.2 gather_fusion.1
  290.6 8.8 %fusion.136 = (f32[4,4,128]{2,1,0:T(4,128)S(1)}, f32[4,4,128,1024]{3,2,1,0:T(8,128)}) fusion(pred[4,1024]{1,0:T(4,128)(4,1)S(1)} %bitcast.204, bf16[4,4,1024,64]{2,1,3,0:T(4,128)(2,1)} %reshape.233, bf16[1,4,4,128,64]{3,2,0,4,1:T(4,128)(2,1)S(1)} %get-tuple-element.244), kind=kOutput, calls=%fused_computation.96.clone.1 | convolution fusion | flops 276825088 | bytes 10760192 | tf_op jit(solution)/shard_map/while/body/eval_jaxpr/sub | solution.py:19
  310.6 5.5 reshape.236
  316.0 5.0 multiply_convert_fusion.2
  328.7 5.5 reshape.235
  351.9 5.2 gather_fusion.2
  364.1 5.2 gather_fusion.1
  376.1 8.8 %fusion.136 = (f32[4,4,128]{2,1,0:T(4,128)S(1)}, f32[4,4,128,1024]{3,2,1,0:T(8,128)}) fusion(pred[4,1024]{1,0:T(4,128)(4,1)S(1)} %bitcast.204, bf16[4,4,1024,64]{2,1,3,0:T(4,128)(2,1)} %reshape.233, bf16[1,4,4,128,64]{3,2,0,4,1:T(4,128)(2,1)S(1)} %get-tuple-element.244), kind=kOutput, calls=%fused_computation.96.clone.1 | convolution fusion | flops 276825088 | bytes 10760192 | tf_op jit(solution)/shard_map/while/body/eval_jaxpr/sub | solution.py:19
  396.1 5.5 reshape.236
  414.2 5.5 reshape.235
  458.0 29.8 %all-to-all-done.3 = bf16[4,16,128,64]{2,3,0,1:T(8,128)(2,1)S(1)} async-done(((bf16[4,16,128,64]{2,3,0,1:T(8,128)(2,1)}), bf16[4,16,128,64]{2,3,0,1:T(8,128)(2,1)S(1)}, u32[]{:S(2)}, u32[]{:S(2)}) %all-to-all-start.3) | async-done | bytes 1048608 | tf_op jit(solution)/shard_map/all_to_all | solution.py:111
  497.6 31.7 %all-to-all-done.4 = bf16[4,16,128,64]{2,3,0,1:T(8,128)(2,1)} async-done(((bf16[4,16,128,64]{2,3,0,1:T(8,128)(2,1)}), bf16[4,16,128,64]{2,3,0,1:T(8,128)(2,1)}, u32[]{:S(2)}, u32[]{:S(2)}) %all-to-all-start.4) | async-done | bytes 1048608 | tf_op jit(solution)/shard_map/all_to_all | solution.py:118
  538.5 5.0 add_add_fusion
  554.5 7.7 %reduce-scatter.12.cloned.1.call-done = f32[256,256]{0,1:T(8,128)} async-done(((f32[1024,256]{0,1:T(8,128)}), f32[256,256]{0,1:T(8,128)}) %reduce-scatter.12.cloned.1.call-update) | async-done | bytes 262160 | tf_op jit(solution)/shard_map/reduce_scatter | solution.py:144
  564.0 71.2 %reduce-scatter.6.cloned.1.call-done = f32[2048,256]{1,0:T(8,128)} async-done(((f32[2048,1024]{1,0:T(8,128)}), f32[2048,256]{1,0:T(8,128)}) %reduce-scatter.6.cloned.1.call-update) | async-done | bytes 2097168 | tf_op jit(solution)/shard_map/reduce_scatter | solution.py:152
  637.9 27.2 %reduce-scatter.14.cloned.1.call-done = f32[256,256]{1,0:T(8,128)} async-done(((f32[256,1024]{1,0:T(8,128)}), f32[256,256]{1,0:T(8,128)}) %reduce-scatter.14.cloned.1.call-update) | async-done | bytes 262160 | tf_op jit(solution)/shard_map/reduce_scatter | solution.py:145
  (271 shorter events, 332.0 us)
Async XLA Ops:
  7.2 67.6 %copy-start = (bf16[1024,256]{1,0:T(8,128)(2,1)S(1)}, bf16[1024,256]{1,0:T(8,128)(2,1)}, u32[]{:S(2)}) copy-start(bf16[1024,256]{1,0:T(8,128)(2,1)} %param.13) | copy-start | bytes 1572868
  7.2 16.7 %all-to-all-start = ((s32[4,1,4]{2,1,0:T(1,128)}), s32[4,1,4]{2,1,0:T(1,128)S(1)}, u32[]{:S(2)}, u32[]{:S(2)}) async-start(s32[4,1,4]{2,1,0:T(1,128)} %bitcast.207), calls=%async_computation | async-start | bytes 4096 | tf_op jit(solution)/shard_map/all_to_all | solution.py:68
  21.5 11.6 %copy-start.13 = (bf16[1024,256]{1,0:T(8,128)(2,1)S(1)}, bf16[1024,256]{1,0:T(8,128)(2,1)}, u32[]{:S(2)}) copy-start(bf16[1024,256]{1,0:T(8,128)(2,1)} %param.14) | copy-start | bytes 1572868
  23.8 13.7 %copy-start.16 = (s32[4,1,4]{2,1,0:T(1,128)}, s32[4,1,4]{2,1,0:T(1,128)S(1)}, u32[]{:S(2)}) copy-start(s32[4,1,4]{2,1,0:T(1,128)S(1)} %all-to-all-done) | copy-start | bytes 196
  28.0 30.4 %all-to-all-start.2 = ((bf16[4,16,128,64]{2,3,0,1:T(8,128)(2,1)}), bf16[4,16,128,64]{2,3,0,1:T(8,128)(2,1)}, u32[]{:S(2)}, u32[]{:S(2)}) async-start(bf16[4,16,128,64]{2,3,0,1:T(8,128)(2,1)} %bitcast.193), calls=%async_computation.2 | async-start | bytes 2097152 | tf_op jit(solution)/shard_map/all_to_all | solution.py:73
  58.4 10.5 %copy-start.22 = (s32[1,4]{1,0:T(1,128)S(1)}, s32[1,4]{1,0:T(1,128)}, u32[]{:S(2)}) copy-start(s32[1,4]{1,0:T(1,128)} %param.18) | copy-start | bytes 52
  58.4 10.6 %copy-start.18 = (s32[16,8]{0,1:T(8,128)S(1)}, s32[16,8]{0,1:T(8,128)}, u32[]{:S(2)}) copy-start(s32[16,8]{0,1:T(8,128)} %param.19) | copy-start | bytes 1540
  58.4 10.7 %copy-start.21 = (bf16[256,1024]{1,0:T(8,128)(2,1)S(1)}, bf16[256,1024]{1,0:T(8,128)(2,1)}, u32[]{:S(2)}) copy-start(bf16[256,1024]{1,0:T(8,128)(2,1)} %param.16) | copy-start | bytes 1572868
  58.4 29.7 %all-to-all-start.1 = ((bf16[4,16,128,64]{2,3,0,1:T(8,128)(2,1)}), bf16[4,16,128,64]{2,3,0,1:T(8,128)(2,1)}, u32[]{:S(2)}, u32[]{:S(2)}) async-start(bf16[4,16,128,64]{2,3,0,1:T(8,128)(2,1)} %bitcast.192), calls=%async_computation.1 | async-start | bytes 2097152 | tf_op jit(solution)/shard_map/all_to_all | solution.py:72
  128.4 4.1 copy-start.7
  145.1 5.0 copy-start.8
  164.0 4.7 copy-start.5
  213.9 4.1 copy-start.7
  230.5 5.0 copy-start.8
  249.5 4.7 copy-start.5
  299.4 4.1 copy-start.7
  316.0 5.0 copy-start.8
  335.0 4.7 copy-start.5
  384.9 4.1 copy-start.7
  401.5 5.0 copy-start.8
  420.5 4.7 copy-start.5
  427.4 3.7 copy-start.3
  444.1 43.7 %all-to-all-start.3 = ((bf16[4,16,128,64]{2,3,0,1:T(8,128)(2,1)}), bf16[4,16,128,64]{2,3,0,1:T(8,128)(2,1)S(1)}, u32[]{:S(2)}, u32[]{:S(2)}) async-start(bf16[4,16,128,64]{2,3,0,1:T(8,128)(2,1)} %slice.35), calls=%async_computation.3 | async-start | bytes 2097152 | tf_op jit(solution)/shard_map/all_to_all | solution.py:111
  447.6 4.5 copy-start.17
  447.6 103.2 %reduce-scatter.8.cloned.1.call-start = ((), (), s32[]{:S(2)}) async-start(), calls=%async_computation.11 | async-start | bytes 1310720 | tf_op jit(solution)/shard_map/reduce_scatter | solution.py:142
  487.8 4.3 copy-start.11
  487.8 41.5 %all-to-all-start.4 = ((bf16[4,16,128,64]{2,3,0,1:T(8,128)(2,1)}), bf16[4,16,128,64]{2,3,0,1:T(8,128)(2,1)}, u32[]{:S(2)}, u32[]{:S(2)}) async-start(bf16[4,16,128,64]{2,3,0,1:T(8,128)(2,1)} %slice.34), calls=%async_computation.4 | async-start | bytes 2097152 | tf_op jit(solution)/shard_map/all_to_all | solution.py:118
  492.1 60.6 %reduce-scatter.10.cloned.1.call-start = ((), (), s32[]{:S(2)}) async-start(), calls=%async_computation.12 | async-start | bytes 1310720 | tf_op jit(solution)/shard_map/reduce_scatter | solution.py:143
  497.6 64.6 %reduce-scatter.12.cloned.1.call-start = ((), (), s32[]{:S(2)}) async-start(), calls=%async_computation.13 | async-start | bytes 1310720 | tf_op jit(solution)/shard_map/reduce_scatter | solution.py:144
  529.3 3.9 copy-start.20
  535.6 99.6 %reduce-scatter.6.cloned.1.call-start = ((), (), s32[]{:S(2)}) async-start(), calls=%async_computation.10 | async-start | bytes 10485760 | tf_op jit(solution)/shard_map/reduce_scatter | solution.py:152
  543.6 121.6 %reduce-scatter.14.cloned.1.call-start = ((), (), s32[]{:S(2)}) async-start(), calls=%async_computation.14 | async-start | bytes 1310720 | tf_op jit(solution)/shard_map/reduce_scatter | solution.py:145
  (25 other events, 59.9 us)
Sparse Core Ops, SparseCore 0:
  452.3 37.6 reduce-scatter.7
  497.7 33.8 reduce-scatter.9
  535.7 26.4 reduce-scatter.11
  564.8 70.3 reduce-scatter.5
  637.9 27.1 reduce-scatter.13
where the time goes:
time: 683 us; the launch traced here: 672 us
  local copies, waits for them, and re-layouts  279 us (41%)
  waiting for transfers between devices  180 us (26%)
  matrix products  150 us (22%)
  starting transfers between devices  24.1 us (4%)
  other arithmetic  23.4 us (3%)
  between operations  14.2 us (2%)
    reduce_scatter x1, waiting for transfers between devices, on_device(): lax.psum_scatter(term_x, 'head', scatter_dimension=1, tiled=True)  71.2 us
    gather x8, local copies, waits for them, and re-layouts, one_step(): value_rows = value_ws[:, flat].reshape(heads, group, kmax * BLOCK, HEAD_DIM)  39.8 us
    gather x8, local copies, waits for them, and re-layouts, one_step(): key_rows = key_ws[:, flat].reshape(heads, group, kmax * BLOCK, HEAD_DIM)  39.8 us
    sub x4, matrix products, softmax_back(): probs = jnp.exp(scores - jnp.max(scores, axis=-1, keepdims=True))  35 us
    all_to_all x1, waiting for transfers between devices, on_device(): lax.all_to_all(acc_v[:, blk_dev:].astype(jnp.bfloat16), 'owner', split_ax...  31.7 us
    all_to_all x1, waiting for transfers between devices, on_device(): lax.all_to_all(acc_k[:, blk_dev:].astype(jnp.bfloat16), 'owner', split_ax...  29.8 us
    while x72, local copies, waits for them, and re-layouts  27.9 us
    reduce_scatter x1, waiting for transfers between devices, on_device(): lax.psum_scatter(term_o, 'owner', scatter_dimension=1, tiled=True)  27.2 us
  transfers between devices with their start and end apart: 10, of which 7 were waited for; matrix products, arithmetic and copies ran while one was open for 14% of the time, Pallas kernels for 0%

commit v1 on v0

v1 whole, which is shorter than its diff:
```python
import functools
import math

import jax
import jax.numpy as jnp
from jax import lax
from jax.experimental import pallas as pl
from jax.experimental.pallas import tpu as pltpu
from jax.sharding import PartitionSpec as P

HEAD_DIM = 64
BLOCK = 128
PAIR = 2 * HEAD_DIM
SCALE = 1.0 / math.sqrt(HEAD_DIM)
EXP2_SCALE = SCALE * math.log2(math.e)


def dot32(a, b):
    return jnp.dot(a, b, preferred_element_type=jnp.float32)


def split_heads(block):
    lane = lax.broadcasted_iota(jnp.int32, block.shape, 1)
    zero = jnp.zeros_like(block)
    return jnp.concatenate(
        [jnp.where(lane < HEAD_DIM, block, zero), jnp.where(lane < HEAD_DIM, zero, block)], axis=0
    )


def split_heads_t(block_t):
    zero = jnp.zeros((HEAD_DIM, BLOCK), block_t.dtype)
    return jnp.concatenate(
        [
            jnp.concatenate([block_t[:HEAD_DIM], zero], axis=1),
            jnp.concatenate([zero, block_t[HEAD_DIM:]], axis=1),
        ],
        axis=0,
    )


def own_columns(product):
    return jnp.concatenate([product[:HEAD_DIM, :BLOCK], product[HEAD_DIM:, BLOCK:]], axis=0)


def attention_back(
    blk_dev,
    kmax,
    pattern_ref,
    alive_ref,
    q_ref,
    g_ref,
    k_own_ref,
    v_own_ref,
    k_far_ref,
    v_far_ref,
    att_ref,
    gq_ref,
    ok_ref,
    ov_ref,
    fk_ref,
    fv_ref,
    k_ws,
    v_ws,
    kt_ws,
    vt_ws,
    acc_k,
    acc_v,
):
    b = pl.program_id(0)
    wset, _, width = k_ws.shape

    @pl.when(b == 0)
    def _():
        k_ws[:blk_dev] = k_own_ref[...]
        v_ws[:blk_dev] = v_own_ref[...]
        k_ws[blk_dev:] = k_far_ref[...]
        v_ws[blk_dev:] = v_far_ref[...]

        def turn(e, carry):
            kt_ws[e] = k_ws[e].T
            vt_ws[e] = v_ws[e].T
            acc_k[e] = jnp.zeros(acc_k.shape[1:], jnp.float32)
            acc_v[e] = jnp.zeros(acc_v.shape[1:], jnp.float32)
            return carry

        lax.fori_loop(0, wset, turn, 0)

    entries = [pattern_ref[b, i] for i in range(kmax)]
    bias = [jnp.where(alive_ref[e] > 0, 0.0, -1e30).astype(jnp.float32) for e in entries]
    for p in range(width // PAIR):
        cols = slice(p * PAIR, (p + 1) * PAIR)
        q = q_ref[:, cols]
        g = g_ref[:, cols]
        q_t = q.T
        g_t = g.T
        keys = jnp.concatenate([k_ws[e, :, cols] for e in entries], axis=0)
        scores = dot32(keys, split_heads_t(q_t))
        tiles = [scores[i * BLOCK : (i + 1) * BLOCK] for i in range(kmax)]
        top = None
        for tile, off in zip(tiles, bias):
            here = jnp.max(tile, axis=0, keepdims=True) * EXP2_SCALE + off
            top = here if top is None else jnp.maximum(top, here)
        tiles = [jnp.exp2(tile * EXP2_SCALE + (off - top)) for tile, off in zip(tiles, bias)]
        total = sum(jnp.sum(tile, axis=0, keepdims=True) for tile in tiles)
        probs = jnp.concatenate(tiles, axis=0) * (1.0 / total)
        probs_low = probs.astype(jnp.bfloat16)
        values_t = jnp.concatenate([vt_ws[e, cols, :] for e in entries], axis=1)
        att_t = own_columns(dot32(values_t, probs_low)).astype(jnp.bfloat16).astype(jnp.float32)
        att_ref[:, cols] = att_t.T.astype(jnp.bfloat16)
        hit = att_t * g_t.astype(jnp.float32)
        row_dot = jnp.concatenate(
            [
                jnp.sum(hit[:HEAD_DIM], axis=0, keepdims=True),
                jnp.sum(hit[HEAD_DIM:], axis=0, keepdims=True),
            ],
            axis=1,
        )
        values = jnp.concatenate([v_ws[e, :, cols] for e in entries], axis=0)
        grad_probs = dot32(values, split_heads_t(g_t))
        grad_scores = (probs * (grad_probs - row_dot)).astype(jnp.bfloat16)
        keys_t = jnp.concatenate([kt_ws[e, cols, :] for e in entries], axis=1)
        gq_t = own_columns(dot32(keys_t, grad_scores)) * SCALE
        gq_ref[:, cols] = gq_t.T.astype(jnp.bfloat16)
        part_k = dot32(grad_scores, split_heads(q))
        part_v = dot32(probs_low, split_heads(g))
        for i, e in enumerate(entries):
            rows = slice(i * BLOCK, (i + 1) * BLOCK)
            acc_k[e, :, cols] += part_k[rows]
            acc_v[e, :, cols] += part_v[rows]

    @pl.when(b == blk_dev - 1)
    def _():
        ok_ref[...] = acc_k[:blk_dev] * SCALE
        ov_ref[...] = acc_v[:blk_dev]
        fk_ref[...] = (acc_k[blk_dev:] * SCALE).astype(jnp.bfloat16)
        fv_ref[...] = acc_v[blk_dev:].astype(jnp.bfloat16)


def attention(pattern, alive, query, grad_attn, k_own, v_own, k_far, v_far):
    blk_dev, kmax = pattern.shape
    width = query.shape[1]
    slots = k_far.shape[0]
    wset = blk_dev + slots
    rows = pl.BlockSpec((BLOCK, width), lambda b, *_: (b, 0))
    whole = lambda n: pl.BlockSpec((n, BLOCK, width), lambda b, *_: (0, 0, 0))
    low = jnp.bfloat16
    full = jnp.float32
    return pl.pallas_call(
        functools.partial(attention_back, blk_dev, kmax),
        grid_spec=pltpu.PrefetchScalarGridSpec(
            num_scalar_prefetch=2,
            grid=(blk_dev,),
            in_specs=[rows, rows, whole(blk_dev), whole(blk_dev), whole(slots), whole(slots)],
            out_specs=[rows, rows, whole(blk_dev), whole(blk_dev), whole(slots), whole(slots)],
            scratch_shapes=[
                pltpu.VMEM((wset, BLOCK, width), low),
                pltpu.VMEM((wset, BLOCK, width), low),
                pltpu.VMEM((wset, width, BLOCK), low),
                pltpu.VMEM((wset, width, BLOCK), low),
                pltpu.VMEM((wset, BLOCK, width), full),
                pltpu.VMEM((wset, BLOCK, width), full),
            ],
        ),
        out_shape=[
            jax.ShapeDtypeStruct(query.shape, low),
            jax.ShapeDtypeStruct(query.shape, low),
            jax.ShapeDtypeStruct((blk_dev, BLOCK, width), full),
            jax.ShapeDtypeStruct((blk_dev, BLOCK, width), full),
            jax.ShapeDtypeStruct((slots, BLOCK, width), low),
            jax.ShapeDtypeStruct((slots, BLOCK, width), low),
        ],
        compiler_params=pltpu.CompilerParams(
            dimension_semantics=("arbitrary",), vmem_limit_bytes=56 * 2**20
        ),
        cost_estimate=pl.CostEstimate(
            flops=12 * blk_dev * BLOCK * kmax * BLOCK * width,
            bytes_accessed=20 * 2**20,
            transcendentals=blk_dev * BLOCK * kmax * BLOCK * (width // HEAD_DIM),
        ),
        name="attention_back",
    )(pattern, alive, query, grad_attn, k_own, v_own, k_far, v_far)


def on_device(tokens, d_out, w_query, w_key, w_value, w_out, fetch_list, fetch_count, pattern):
    blk_dev, kmax = pattern.shape
    cap = fetch_list.shape[2]
    width = w_query.shape[1]
    rows = tokens.shape[0]
    across = (((1,), (1,)), ((), ()))
    down = (((0,), (0,)), ((), ()))
    low = jnp.bfloat16
    swap = functools.partial(
        lax.all_to_all, axis_name="owner", split_axis=0, concat_axis=0, tiled=True
    )
    wanted = swap(fetch_list[0]).reshape(-1)
    keys_own = dot32(tokens, w_key).astype(low).reshape(blk_dev, BLOCK, width)
    k_far = swap(keys_own[wanted])
    values_own = dot32(tokens, w_value).astype(low).reshape(blk_dev, BLOCK, width)
    v_far = swap(values_own[wanted])
    query = dot32(tokens, w_query).astype(low)
    grad_attn = lax.dot_general(d_out, w_out, across, preferred_element_type=jnp.float32).astype(low)
    live = (jnp.arange(cap, dtype=jnp.int32)[None, :] < fetch_count[0][:, None]).reshape(-1)
    alive = jnp.concatenate([jnp.ones((blk_dev,), jnp.int32), live.astype(jnp.int32)])
    attended, grad_q, own_k, own_v, far_k, far_v = attention(
        pattern, alive, query, grad_attn, keys_own, values_own, k_far, v_far
    )
    back_k = swap(far_k)
    back_v = swap(far_v)
    term_o = lax.dot_general(attended, d_out, down, preferred_element_type=jnp.float32)
    term_q = lax.dot_general(tokens, grad_q, down, preferred_element_type=jnp.float32)
    owned = (jnp.arange(blk_dev, dtype=jnp.int32)[:, None] == wanted[None, :]).astype(low)

    def collect(own, back):
        far = jnp.einsum("ek,kbd->ebd", owned, back, preferred_element_type=jnp.float32)
        return (own + far).astype(low).reshape(rows, width)

    grad_k = collect(own_k, back_k)
    grad_v = collect(own_v, back_v)
    term_k = lax.dot_general(tokens, grad_k, down, preferred_element_type=jnp.float32)
    term_v = lax.dot_general(tokens, grad_v, down, preferred_element_type=jnp.float32)

    def owner_sum(term, axis):
        return lax.psum_scatter(
            term.astype(low), "owner", scatter_dimension=axis, tiled=True
        ).astype(jnp.float32)

    term_x = (
        lax.dot_general(grad_q, w_query, across, preferred_element_type=jnp.float32)
        + lax.dot_general(grad_k, w_key, across, preferred_element_type=jnp.float32)
        + lax.dot_general(grad_v, w_value, across, preferred_element_type=jnp.float32)
    )
    d_tokens = lax.psum_scatter(term_x.astype(low), "head", scatter_dimension=1, tiled=True)
    return (
        d_tokens,
        owner_sum(term_q, 0),
        owner_sum(term_k, 0),
        owner_sum(term_v, 0),
        owner_sum(term_o, 1),
    )


def solution(mesh):
    placed = (
        P(("groups", "owner"), None),
        P(("groups", "owner"), None),
        P(None, "head"),
        P(None, "head"),
        P(None, "head"),
        P("head", None),
        P(("groups", "owner"), None, None),
        P(("groups", "owner"), None),
        P(("groups", "owner"), None),
    )
    return jax.shard_map(
        on_device,
        mesh=mesh,
        in_specs=placed,
        out_specs=(
            P(("groups", "owner"), "head"),
            P(("groups", "owner"), "head"),
            P(("groups", "owner"), "head"),
            P(("groups", "owner"), "head"),
            P(("groups", "head"), "owner"),
        ),
        check_vma=False,
    )
```

time: 683 us -> 314 us (0.46); the launches traced: 672 us -> 314 us
  local copies, waits for them, and re-layouts: 279 us -> 11.8 us
  matrix products: 150 us -> 42.9 us
  Pallas kernels: 0 us -> 61.8 us
  waiting for transfers between devices: 180 us -> 155 us
  other arithmetic: 23.4 us -> 5.69 us
    gather x22 -> x2, local copies, waits for them, and re-layouts: 88.3 us -> 3.19 us  [the longest x1 1.6 us: on_device(): v_far = swap(values_own[wanted])]
    reshape x33 -> x1, local copies, waits for them, and re-layouts: 80.3 us -> 0.09 us  [on_device(): wanted = swap(fetch_list[0]).reshape(-1)]
    dot_general x41 -> x5, matrix products: 90.7 us -> 14.6 us  [the longest x3 11.8 us: dot32(): return jnp.dot(a, b, preferred_element_type=jnp.float32)]
    pallas_call x0 -> x1, Pallas kernels: none -> 61.8 us  [attention(): pl.pallas_call(functools.partial(attention_back, blk_dev, kmax), grid_spe...]
    reduce_scatter x5, waiting for transfers between devices: 106 us -> 69 us  [the longest x1 44.1 us: on_device(): lax.psum_scatter(term_x.astype(low), 'head', scatter_dimension=1, tiled=T...]
    while x74 -> x0, local copies, waits for them, and re-layouts: 37.2 us -> none
    sub x4 -> x0, matrix products: 35 us -> none  [softmax_back(): probs = jnp.exp(scores - jnp.max(scores, axis=-1, keepdims=True))]
    dot_general x4 -> x0, local copies, waits for them, and re-layouts: 18.6 us -> none  [softmax_back(): jnp.einsum('hgts,hgtd->hgsd', probs_low, grad_grp, preferred_element_type...]
  transfers between devices with their start and end apart: 10 -> 10, of which waited for: 7 -> 8; matrix products, arithmetic and copies ran while one was open for 14% -> 18% of each run, Pallas kernels for 0% -> 0%
where the time goes in v1:
time: 314 us
  waiting for transfers between devices  155 us (49%)
  Pallas kernels  61.8 us (20%)
  matrix products  42.9 us (14%)
  starting transfers between devices  22.4 us (7%)
  between operations  14 us (4%)
  local copies, waits for them, and re-layouts  11.8 us (4%)
  other arithmetic  5.69 us (2%)
    pallas_call x1, Pallas kernels, attention(): pl.pallas_call(functools.partial(attention_back, blk_dev, kmax), grid_spe...  61.8 us
    reduce_scatter x1, waiting for transfers between devices, on_device(): lax.psum_scatter(term_x.astype(low), 'head', scatter_dimension=1, tiled=T...  44.1 us
    all_to_all x1, waiting for transfers between devices, on_device(): back_v = swap(far_v)  28.8 us
    reduce_scatter x4, waiting for transfers between devices, owner_sum(): lax.psum_scatter(term.astype(low), 'owner', scatter_dimension=axis, tiled...  24.9 us
    all_to_all x1, waiting for transfers between devices, on_device(): k_far = swap(keys_own[wanted])  19.5 us
    all_to_all x1, waiting for transfers between devices, on_device(): back_k = swap(far_k)  19.4 us
    all_to_all x1, waiting for transfers between devices, on_device(): v_far = swap(values_own[wanted])  16.7 us
    dot_general x3, matrix products, dot32(): return jnp.dot(a, b, preferred_element_type=jnp.float32)  11.8 us
  transfers between devices with their start and end apart: 10, of which 8 were waited for; matrix products, arithmetic and copies ran while one was open for 18% of the time, Pallas kernels for 0%

profile of v1, /device:TPU:0, one launch (start us, length us, event | category | flops | bytes accessed | tf_op | source)
XLA Modules:
  0.0 313.9 jit_solution(8258999654072693247)
XLA Ops:
  7.2 6.5 %all-to-all-start = ((s32[4,1,4]{2,1,0:T(1,128)}), s32[4,1,4]{2,1,0:T(1,128)S(1)}, u32[]{:S(2)}, u32[]{:S(2)}) async-start(s32[4,1,4]{2,1,0:T(1,128)} %bitcast.52), calls=%async_computation | async-start | bytes 4096 | tf_op jit(solution)/shard_map/all_to_all | solution.py:195
  13.6 3.6 %convolution_convert_fusion.1 = bf16[2048,256]{1,0:T(8,128)(2,1)S(1)} fusion(bf16[2048,1024]{1,0:T(8,128)(2,1)} %param.9, bf16[1024,256]{1,0:T(8,128)(2,1)} %param.12), kind=kOutput, calls=%fused_computation.4 | convolution fusion | flops 1074266112 | bytes 5767168 | tf_op jit(solution)/shard_map/dot_general | solution.py:19
  17.3 1.8 all-to-all-done
  20.4 1.6 gather_fusion
  22.0 4.2 %all-to-all-start.1 = ((bf16[16,128,256]{2,1,0:T(8,128)(2,1)}), bf16[16,128,256]{2,1,0:T(8,128)(2,1)}, u32[]{:S(2)}, u32[]{:S(2)}) async-start(bf16[16,128,256]{2,1,0:T(8,128)(2,1)} %gather_fusion), calls=%async_computation.1 | async-start | bytes 2097152 | tf_op jit(solution)/shard_map/all_to_all | solution.py:197
  26.3 3.4 %convolution_convert_fusion = bf16[2048,256]{1,0:T(8,128)(2,1)S(1)} fusion(bf16[2048,1024]{1,0:T(8,128)(2,1)} %param.9, bf16[1024,256]{1,0:T(8,128)(2,1)S(1)} %copy-done.8), kind=kOutput, calls=%fused_computation.3 | convolution fusion | flops 1074266112 | bytes 5767168 | tf_op jit(solution)/shard_map/dot_general | solution.py:19
  29.7 1.6 gather_fusion.1
  31.3 19.5 %all-to-all-done.1.k_far_ref = bf16[16,128,256]{2,1,0:T(8,128)(2,1)} async-done(((bf16[16,128,256]{2,1,0:T(8,128)(2,1)}), bf16[16,128,256]{2,1,0:T(8,128)(2,1)}, u32[]{:S(2)}, u32[]{:S(2)}) %all-to-all-start.1) | async-done | bytes 1048608 | tf_op jit(solution)/shard_map/all_to_all | solution.py:197
  50.9 3.5 %all-to-all-start.2 = ((bf16[16,128,256]{2,1,0:T(8,128)(2,1)}), bf16[16,128,256]{2,1,0:T(8,128)(2,1)S(1)}, u32[]{:S(2)}, u32[]{:S(2)}) async-start(bf16[16,128,256]{2,1,0:T(8,128)(2,1)} %gather_fusion.1), calls=%async_computation.2 | async-start | bytes 2097152 | tf_op jit(solution)/shard_map/all_to_all | solution.py:199
  55.8 4.7 %convolution_convert_fusion.3.q_ref = bf16[2048,256]{1,0:T(8,128)(2,1)} fusion(bf16[2048,1024]{1,0:T(8,128)(2,1)} %param.9, bf16[1024,256]{1,0:T(8,128)(2,1)S(1)} %copy-done), kind=kOutput, calls=%fused_computation.6 | convolution fusion | flops 1074266112 | bytes 5767168 | tf_op jit(solution)/shard_map/dot_general | solution.py:19
  60.6 2.3 convolution_convert_fusion.2.g_ref
  62.8 16.7 %all-to-all-done.2.v_far_ref = bf16[16,128,256]{2,1,0:T(8,128)(2,1)S(1)} async-done(((bf16[16,128,256]{2,1,0:T(8,128)(2,1)}), bf16[16,128,256]{2,1,0:T(8,128)(2,1)S(1)}, u32[]{:S(2)}, u32[]{:S(2)}) %all-to-all-start.2) | async-done | bytes 1048608 | tf_op jit(solution)/shard_map/all_to_all | solution.py:199
  80.6 61.8 %attention_back.1 = (bf16[2048,256]{1,0:T(8,128)(2,1)}, bf16[2048,256]{1,0:T(8,128)(2,1)}, f32[16,128,256]{2,1,0:T(8,128)}, f32[16,128,256]{2,1,0:T(8,128)}, bf1...) custom-call(s32[16,8]{1,0:T(8,128)} %copy.23.pattern_ref, s32[32]{0:T(128)} %pad_convert_fusion.alive_ref, ...), custom_call_target="tpu_custom_call" | custom-call | flops 6442450944 | bytes 20971520 | tf_op jit(solution)/shard_map/attention_back/pallas_call | solution.py:148
  142.4 3.5 %all-to-all-start.4 = ((bf16[16,128,256]{2,1,0:T(8,128)(2,1)}), bf16[16,128,256]{2,1,0:T(8,128)(2,1)S(1)}, u32[]{:S(2)}, u32[]{:S(2)}) async-start(bf16[16,128,256]{2,1,0:T(8,128)(2,1)} %get-tuple-element.15), calls=%async_computation.4 | async-start | bytes 2097152 | tf_op jit(solution)/shard_map/all_to_all | solution.py:208
  146.0 4.7 %convolution_convert_fusion.4 = bf16[256,1024]{1,0:T(8,128)(2,1)} fusion(bf16[2048,256]{1,0:T(8,128)(2,1)} %get-tuple-element.16, bf16[2048,1024]{1,0:T(8,128)(2,1)} %param.10), kind=kOutput, calls=%fused_computation.11 | convolution fusion | flops 1074003968 | bytes 5767168 | tf_op jit(solution)/shard_map/dot_general | solution.py:209
  150.8 28.8 %all-to-all-done.4 = bf16[16,128,256]{2,1,0:T(8,128)(2,1)S(1)} async-done(((bf16[16,128,256]{2,1,0:T(8,128)(2,1)}), bf16[16,128,256]{2,1,0:T(8,128)(2,1)S(1)}, u32[]{:S(2)}, u32[]{:S(2)}) %all-to-all-start.4) | async-done | bytes 1048608 | tf_op jit(solution)/shard_map/all_to_all | solution.py:208
  179.5 4.3 %all-to-all-start.3 = ((bf16[16,128,256]{2,1,0:T(8,128)(2,1)}), bf16[16,128,256]{2,1,0:T(8,128)(2,1)}, u32[]{:S(2)}, u32[]{:S(2)}) async-start(bf16[16,128,256]{2,1,0:T(8,128)(2,1)} %get-tuple-element.13), calls=%async_computation.3 | async-start | bytes 2097152 | tf_op jit(solution)/shard_map/all_to_all | solution.py:207
  183.9 4.3 %fusion.2 = bf16[1024,256]{0,1:T(8,128)(2,1)} fusion(bf16[2048,256]{1,0:T(8,128)(2,1)S(1)} %copy-done.3, bf16[2048,1024]{1,0:T(8,128)(2,1)} %param.9), kind=kOutput, calls=%fused_computation.15 | convolution fusion | flops 1074003968 | bytes 5767168 | tf_op jit(solution)/shard_map/dot_general | solution.py:210
  188.4 4.5 %fusion.15 = f32[2048,1024]{1,0:T(8,128)} fusion(bf16[2048,256]{1,0:T(8,128)(2,1)S(1)} %copy-done.3, bf16[1024,256]{1,0:T(8,128)(2,1)S(1)} %copy-done), kind=kOutput, calls=%fused_computation.31 | convolution fusion | flops 1073741824 | bytes 9961472 | tf_op jit(solution)/shard_map/dot_general | solution.py:228
  195.9 2.1 fusion.4
  198.1 19.4 %all-to-all-done.3 = bf16[16,128,256]{2,1,0:T(8,128)(2,1)} async-done(((bf16[16,128,256]{2,1,0:T(8,128)(2,1)}), bf16[16,128,256]{2,1,0:T(8,128)(2,1)}, u32[]{:S(2)}, u32[]{:S(2)}) %all-to-all-start.3) | async-done | bytes 1048608 | tf_op jit(solution)/shard_map/all_to_all | solution.py:207
  217.5 2.1 fusion.7
  219.6 1.4 fusion.1
  221.0 2.1 fusion.3
  224.5 7.0 %add_convert_fusion = bf16[2048,1024]{1,0:T(8,128)(2,1)} fusion(f32[2048,1024]{1,0:T(8,128)} %fusion.15, f32[2048,1024]{1,0:T(8,128)S(1)} %fusion.16, bf16[2048,256]{1,0:T(8,128)(2,1)S(1)} %bitcast.46, bf16[1024,256]{1,0:T(8,128)(2,1)S(1)} %copy-done.9), kind=kOutput, calls=%fused_computation.2 | convolution fusion | flops 1080033280 | bytes 22544384 | tf_op jit(solution)/shard_map/dot_general | solution.py:230
  231.6 1.6 convert_element_type.77
  233.2 1.7 copy.28
  234.9 4.5 %reduce-scatter.12.cloned.1.call-done = bf16[256,256]{0,1:T(8,128)(2,1)} async-done(((bf16[1024,256]{0,1:T(8,128)(2,1)}), bf16[256,256]{0,1:T(8,128)(2,1)}) %reduce-scatter.12.cloned.1.call-update) | async-done | bytes 131088 | tf_op jit(solution)/shard_map/reduce_scatter | solution.py:223
  239.4 1.7 copy.30
  241.2 20.3 %reduce-scatter.10.cloned.1.call-done = bf16[256,256]{0,1:T(8,128)(2,1)} async-done(((bf16[1024,256]{0,1:T(8,128)(2,1)}), bf16[256,256]{0,1:T(8,128)(2,1)}) %reduce-scatter.10.cloned.1.call-update) | async-done | bytes 131088 | tf_op jit(solution)/shard_map/reduce_scatter | solution.py:223
  261.5 1.7 copy.29
  263.2 44.1 %reduce-scatter.6.cloned.1.call-done = bf16[2048,256]{1,0:T(8,128)(2,1)} async-done(((bf16[2048,1024]{1,0:T(8,128)(2,1)}), bf16[2048,256]{1,0:T(8,128)(2,1)}) %reduce-scatter.6.cloned.1.call-update) | async-done | bytes 1048592 | tf_op jit(solution)/shard_map/reduce_scatter | solution.py:232
  (57 shorter events, 8.6 us)
Async XLA Ops:
  7.2 48.7 %copy-start = (bf16[1024,256]{1,0:T(8,128)(2,1)S(1)}, bf16[1024,256]{1,0:T(8,128)(2,1)}, u32[]{:S(2)}) copy-start(bf16[1024,256]{1,0:T(8,128)(2,1)} %param.11) | copy-start | bytes 1572868
  7.2 11.9 %all-to-all-start = ((s32[4,1,4]{2,1,0:T(1,128)}), s32[4,1,4]{2,1,0:T(1,128)S(1)}, u32[]{:S(2)}, u32[]{:S(2)}) async-start(s32[4,1,4]{2,1,0:T(1,128)} %bitcast.52), calls=%async_computation | async-start | bytes 4096 | tf_op jit(solution)/shard_map/all_to_all | solution.py:195
  13.6 12.6 %copy-start.8 = (bf16[1024,256]{1,0:T(8,128)(2,1)S(1)}, bf16[1024,256]{1,0:T(8,128)(2,1)}, u32[]{:S(2)}) copy-start(bf16[1024,256]{1,0:T(8,128)(2,1)} %param.13) | copy-start | bytes 1572868
  17.3 12.5 %copy-start.4 = (bf16[2048,256]{1,0:T(8,128)(2,1)}, bf16[2048,256]{1,0:T(8,128)(2,1)S(1)}, u32[]{:S(2)}) copy-start(bf16[2048,256]{1,0:T(8,128)(2,1)S(1)} %convolution_convert_fusion.1) | copy-start | bytes 3145732
  22.0 28.9 %all-to-all-start.1 = ((bf16[16,128,256]{2,1,0:T(8,128)(2,1)}), bf16[16,128,256]{2,1,0:T(8,128)(2,1)}, u32[]{:S(2)}, u32[]{:S(2)}) async-start(bf16[16,128,256]{2,1,0:T(8,128)(2,1)} %gather_fusion), calls=%async_computation.1 | async-start | bytes 2097152 | tf_op jit(solution)/shard_map/all_to_all | solution.py:197
  26.2 28.2 %copy-start.15 = (s32[1,4]{1,0:T(1,128)S(1)}, s32[1,4]{1,0:T(1,128)}, u32[]{:S(2)}) copy-start(s32[1,4]{1,0:T(1,128)} %param.16) | copy-start | bytes 52
  26.3 28.3 %copy-start.10 = (s32[16,8]{0,1:T(8,128)S(1)}, s32[16,8]{0,1:T(8,128)}, u32[]{:S(2)}) copy-start(s32[16,8]{0,1:T(8,128)} %param.17) | copy-start | bytes 1540
  29.7 30.8 %copy-start.5 = (bf16[2048,256]{1,0:T(8,128)(2,1)}, bf16[2048,256]{1,0:T(8,128)(2,1)S(1)}, u32[]{:S(2)}) copy-start(bf16[2048,256]{1,0:T(8,128)(2,1)S(1)} %convolution_convert_fusion) | copy-start | bytes 3145732
  50.9 28.7 %all-to-all-start.2 = ((bf16[16,128,256]{2,1,0:T(8,128)(2,1)}), bf16[16,128,256]{2,1,0:T(8,128)(2,1)S(1)}, u32[]{:S(2)}, u32[]{:S(2)}) async-start(bf16[16,128,256]{2,1,0:T(8,128)(2,1)} %gather_fusion.1), calls=%async_computation.2 | async-start | bytes 2097152 | tf_op jit(solution)/shard_map/all_to_all | solution.py:199
  54.4 6.2 %copy-start.14 = (bf16[256,1024]{1,0:T(8,128)(2,1)S(1)}, bf16[256,1024]{1,0:T(8,128)(2,1)}, u32[]{:S(2)}) copy-start(bf16[256,1024]{1,0:T(8,128)(2,1)} %param.14) | copy-start | bytes 1572868
  55.2 5.3 %copy-start.11 = (bf16[2048,1024]{1,0:T(8,128)(2,1)S(1)}, bf16[2048,1024]{1,0:T(8,128)(2,1)}, u32[]{:S(2)}) copy-start(bf16[2048,1024]{1,0:T(8,128)(2,1)} %param.10) | copy-start | bytes 12582916
  79.6 1.1 copy-start.6
  142.4 37.1 %all-to-all-start.4 = ((bf16[16,128,256]{2,1,0:T(8,128)(2,1)}), bf16[16,128,256]{2,1,0:T(8,128)(2,1)S(1)}, u32[]{:S(2)}, u32[]{:S(2)}) async-start(bf16[16,128,256]{2,1,0:T(8,128)(2,1)} %get-tuple-element.15), calls=%async_computation.4 | async-start | bytes 2097152 | tf_op jit(solution)/shard_map/all_to_all | solution.py:208
  145.9 85.7 %reduce-scatter.14.cloned.1.call-start = ((), (), s32[]{:S(2)}) async-start(), calls=%async_computation.14 | async-start | bytes 655360 | tf_op jit(solution)/shard_map/reduce_scatter | solution.py:223
  146.0 37.9 %copy-start.3 = (bf16[2048,256]{1,0:T(8,128)(2,1)S(1)}, bf16[2048,256]{1,0:T(8,128)(2,1)}, u32[]{:S(2)}) copy-start(bf16[2048,256]{1,0:T(8,128)(2,1)} %get-tuple-element.11) | copy-start | bytes 3145732
  179.5 38.0 %all-to-all-start.3 = ((bf16[16,128,256]{2,1,0:T(8,128)(2,1)}), bf16[16,128,256]{2,1,0:T(8,128)(2,1)}, u32[]{:S(2)}, u32[]{:S(2)}) async-start(bf16[16,128,256]{2,1,0:T(8,128)(2,1)} %get-tuple-element.13), calls=%async_computation.3 | async-start | bytes 2097152 | tf_op jit(solution)/shard_map/all_to_all | solution.py:207
  183.8 49.4 %reduce-scatter.8.cloned.1.call-start = ((), (), s32[]{:S(2)}) async-start(), calls=%async_computation.11 | async-start | bytes 655360 | tf_op jit(solution)/shard_map/reduce_scatter | solution.py:223
  188.2 51.3 %reduce-scatter.12.cloned.1.call-start = ((), (), s32[]{:S(2)}) async-start(), calls=%async_computation.13 | async-start | bytes 655360 | tf_op jit(solution)/shard_map/reduce_scatter | solution.py:223
  193.0 1.6 copy-start.2
  193.0 3.0 copy-start.12
  198.0 63.5 %reduce-scatter.10.cloned.1.call-start = ((), (), s32[]{:S(2)}) async-start(), calls=%async_computation.12 | async-start | bytes 655360 | tf_op jit(solution)/shard_map/reduce_scatter | solution.py:223
  217.5 2.1 copy-start.1
  217.5 3.5 %copy-start.13 = (bf16[2048,1024]{1,0:T(8,128)(2,1)S(1)}, bf16[2048,1024]{1,0:T(8,128)(2,1)}, u32[]{:S(2)}) copy-start(bf16[2048,1024]{1,0:T(8,128)(2,1)} %param.9) | copy-start | bytes 12582916
  221.0 2.2 copy-start.7
  223.1 84.2 %reduce-scatter.6.cloned.1.call-start = ((), (), s32[]{:S(2)}) async-start(), calls=%async_computation.10 | async-start | bytes 5242880 | tf_op jit(solution)/shard_map/reduce_scatter | solution.py:232
  223.2 1.3 copy-start.9
Sparse Core Ops, SparseCore 0:
  150.8 27.7 reduce-scatter.13
  188.3 28.1 reduce-scatter.7
  218.8 20.5 reduce-scatter.11
  241.6 19.8 reduce-scatter.9
  264.4 42.8 reduce-scatter.5

commit v2 on v1

--- a/solution.py
+++ b/solution.py
@@ -181,6 +181,164 @@
     )(pattern, alive, query, grad_attn, k_own, v_own, k_far, v_far)
 
 
+CHUNKS = 4
+TERMS = 4
+MESH_ID = pl.DeviceIdType.MESH
+
+
+def finish_sums(owners, heads, *refs):
+    terms, (gq_ref, gk_ref, gv_ref, wq_ref, wk_ref, wv_ref) = refs[:TERMS], refs[TERMS : TERMS + 6]
+    sums, dx_ref = refs[TERMS + 6 : 2 * TERMS + 6], refs[2 * TERMS + 6]
+    (x_ref, near, mixed, far, got, near_send, near_recv, far_send, far_recv, got_send, got_recv) = refs[
+        2 * TERMS + 7 :
+    ]
+    chips = heads // 2
+    owner = lax.axis_index("owner")
+    head = lax.axis_index("head")
+    chip, core = head // 2, head % 2
+    partner = chip * 2 + (1 - core)
+    part = terms[0].shape[0] // owners
+    rows, cols = dx_ref.shape
+    step = rows // CHUNKS
+
+    barrier = pltpu.get_barrier_semaphore()
+    for off in range(1, owners):
+        pl.semaphore_signal(
+            barrier, inc=1, device_id={"owner": lax.rem(owner + off, owners)}, device_id_type=MESH_ID
+        )
+    pl.semaphore_signal(barrier, inc=1, device_id={"head": partner}, device_id_type=MESH_ID)
+    for off in range(1, chips):
+        pl.semaphore_signal(
+            barrier,
+            inc=1,
+            device_id={"head": lax.rem(chip + off, chips) * 2 + core},
+            device_id_type=MESH_ID,
+        )
+    pl.semaphore_wait(barrier, owners - 1 + 1 + chips - 1)
+
+    sends = []
+    for t in range(TERMS):
+        for off in range(1, owners):
+            to = lax.rem(owner + off, owners)
+            copy = pltpu.make_async_remote_copy(
+                src_ref=terms[t].at[pl.ds(pl.multiple_of(to * part, part), part)],
+                dst_ref=got.at[t, off - 1],
+                send_sem=got_send.at[t, off - 1],
+                recv_sem=got_recv.at[t, off - 1],
+                device_id={"owner": to},
+                device_id_type=MESH_ID,
+            )
+            copy.start()
+            sends.append(copy)
+
+    weights = jnp.concatenate([wq_ref[...], wk_ref[...], wv_ref[...]], axis=1)
+    near_copies = []
+    for c in range(CHUNKS):
+        here = slice(c * step, (c + 1) * step)
+        grads = jnp.concatenate([gq_ref[here], gk_ref[here], gv_ref[here]], axis=1)
+        for h in range(heads):
+            x_ref[h, here] = lax.dot_general(
+                grads,
+                weights[h * cols : (h + 1) * cols],
+                (((1,), (1,)), ((), ())),
+                preferred_element_type=jnp.float32,
+            ).astype(jnp.bfloat16)
+        copies = []
+        for j in range(chips):
+            copy = pltpu.make_async_remote_copy(
+                src_ref=x_ref.at[j * 2 + (1 - core), pl.ds(c * step, step)],
+                dst_ref=near.at[j, pl.ds(c * step, step)],
+                send_sem=near_send.at[c, j],
+                recv_sem=near_recv.at[c, j],
+                device_id={"head": partner},
+                device_id_type=MESH_ID,
+            )
+            copy.start()
+            copies.append(copy)
+        near_copies.append(copies)
+
+    far_copies = []
+    for c in range(CHUNKS):
+        here = slice(c * step, (c + 1) * step)
+        for copy in near_copies[c]:
+            copy.wait_recv()
+        copies = []
+        for off in range(1, chips):
+            to = lax.rem(chip + off, chips)
+            mixed[off - 1, here] = (
+                x_ref[to * 2 + core, here].astype(jnp.float32)
+                + near[to, here].astype(jnp.float32)
+            ).astype(jnp.bfloat16)
+            copy = pltpu.make_async_remote_copy(
+                src_ref=mixed.at[off - 1, pl.ds(c * step, step)],
+                dst_ref=far.at[off - 1, pl.ds(c * step, step)],
+                send_sem=far_send.at[c, off - 1],
+                recv_sem=far_recv.at[c, off - 1],
+                device_id={"head": to * 2 + core},
+                device_id_type=MESH_ID,
+            )
+            copy.start()
+            copies.append(copy)
+        far_copies.append(copies)
+
+    for c in range(CHUNKS):
+        here = slice(c * step, (c + 1) * step)
+        total = x_ref[head, here].astype(jnp.float32) + near[chip, here].astype(jnp.float32)
+        for off, copy in enumerate(far_copies[c]):
+            copy.wait_recv()
+            total += far[off, here].astype(jnp.float32)
+        dx_ref[here] = total.astype(jnp.bfloat16)
+    for t in range(TERMS):
+        total = terms[t][pl.ds(pl.multiple_of(owner * part, part), part)].astype(jnp.float32)
+        for off in range(owners - 1):
+            sends[t * (owners - 1) + off].wait_recv()
+            total += got[t, off].astype(jnp.float32)
+        sums[t][...] = total
+    for copy in sends:
+        copy.wait_send()
+    for copies in near_copies + far_copies:
+        for copy in copies:
+            copy.wait_send()
+
+
+def finish(terms, grads, weights):
+    owners = lax.axis_size("owner")
+    heads = lax.axis_size("head")
+    chips = heads // 2
+    depth, width = terms[0].shape
+    rows = grads[0].shape[0]
+    part, cols = depth // owners, depth // heads
+    low = jnp.bfloat16
+    vmem = pl.BlockSpec(memory_space=pltpu.VMEM)
+    return pl.pallas_call(
+        functools.partial(finish_sums, owners, heads),
+        out_shape=[jax.ShapeDtypeStruct((part, width), jnp.float32)] * TERMS
+        + [jax.ShapeDtypeStruct((rows, cols), low)],
+        in_specs=[vmem] * (TERMS + 6),
+        out_specs=[vmem] * (TERMS + 1),
+        scratch_shapes=[
+            pltpu.VMEM((heads, rows, cols), low),
+            pltpu.VMEM((chips, rows, cols), low),
+            pltpu.VMEM((chips - 1, rows, cols), low),
+            pltpu.VMEM((chips - 1, rows, cols), low),
+            pltpu.VMEM((TERMS, owners - 1, part, width), low),
+            pltpu.SemaphoreType.DMA((CHUNKS, chips)),
+            pltpu.SemaphoreType.DMA((CHUNKS, chips)),
+            pltpu.SemaphoreType.DMA((CHUNKS, chips - 1)),
+            pltpu.SemaphoreType.DMA((CHUNKS, chips - 1)),
+            pltpu.SemaphoreType.DMA((TERMS, owners - 1)),
+            pltpu.SemaphoreType.DMA((TERMS, owners - 1)),
+        ],
+        compiler_params=pltpu.CompilerParams(
+            collective_id=0, has_side_effects=True, vmem_limit_bytes=48 * 2**20
+        ),
+        cost_estimate=pl.CostEstimate(
+            flops=6 * rows * depth * width, bytes_accessed=10 * 2**20, transcendentals=0
+        ),
+        name="finish_sums",
+    )(*terms, *grads, *weights)
+
+
 def on_device(tokens, d_out, w_query, w_key, w_value, w_out, fetch_list, fetch_count, pattern):
     blk_dev, kmax = pattern.shape
     cap = fetch_list.shape[2]
@@ -206,8 +364,11 @@
     )
     back_k = swap(far_k)
     back_v = swap(far_v)
-    term_o = lax.dot_general(attended, d_out, down, preferred_element_type=jnp.float32)
-    term_q = lax.dot_general(tokens, grad_q, down, preferred_element_type=jnp.float32)
+    def term(left, right):
+        return lax.dot_general(left, right, down, preferred_element_type=jnp.float32).astype(low)
+
+    term_o = term(d_out, attended)
+    term_q = term(tokens, grad_q)
     owned = (jnp.arange(blk_dev, dtype=jnp.int32)[:, None] == wanted[None, :]).astype(low)
 
     def collect(own, back):
@@ -216,27 +377,11 @@
 
     grad_k = collect(own_k, back_k)
     grad_v = collect(own_v, back_v)
-    term_k = lax.dot_general(tokens, grad_k, down, preferred_element_type=jnp.float32)
-    term_v = lax.dot_general(tokens, grad_v, down, preferred_element_type=jnp.float32)
-
-    def owner_sum(term, axis):
-        return lax.psum_scatter(
-            term.astype(low), "owner", scatter_dimension=axis, tiled=True
-        ).astype(jnp.float32)
-
-    term_x = (
-        lax.dot_general(grad_q, w_query, across, preferred_element_type=jnp.float32)
-        + lax.dot_general(grad_k, w_key, across, preferred_element_type=jnp.float32)
-        + lax.dot_general(grad_v, w_value, across, preferred_element_type=jnp.float32)
-    )
-    d_tokens = lax.psum_scatter(term_x.astype(low), "head", scatter_dimension=1, tiled=True)
-    return (
-        d_tokens,
-        owner_sum(term_q, 0),
-        owner_sum(term_k, 0),
-        owner_sum(term_v, 0),
-        owner_sum(term_o, 1),
-    )
+    terms = (term_q, term(tokens, grad_k), term(tokens, grad_v), term_o)
+    sum_q, sum_k, sum_v, sum_o, d_tokens = finish(
+        terms, (grad_q, grad_k, grad_v), (w_query, w_key, w_value)
+    )
+    return (d_tokens, sum_q, sum_k, sum_v, sum_o.T)
 
 
 def solution(mesh):

time: 314 us -> 252 us (0.80)
  waiting for transfers between devices: 155 us -> 72.4 us
  Pallas kernels: 61.8 us -> 110 us
  between operations: 14 us -> 0.91 us
  matrix products: 42.9 us -> 30.1 us
    reduce_scatter x5 -> x0, waiting for transfers between devices: 69 us -> none  [the longest x1 44.1 us: on_device(): lax.psum_scatter(term_x.astype(low), 'head', scatter_dimension=1, tiled=T...]
    pallas_call x0 -> x1, Pallas kernels: none -> 48.1 us  [finish(): pl.pallas_call(functools.partial(finish_sums, owners, heads), out_shape=[...]
    dot_general x7 -> x4, matrix products: 26 us -> 12.2 us  [term(): lax.dot_general(left, right, down, preferred_element_type=jnp.float32)]
    all_to_all x1, waiting for transfers between devices: 19.4 us -> 11.5 us  [on_device(): back_k = swap(far_k)]
    all_to_all x1, waiting for transfers between devices: 28.8 us -> 25.1 us  [on_device(): back_v = swap(far_v)]
    unnamed x36 -> x50, local copies, waits for them, and re-layouts: 7.8 us -> 6.87 us
  transfers between devices with their start and end apart: 10 -> 5, of which waited for: 8 -> 5; matrix products, arithmetic and copies ran while one was open for 18% -> 13% of each run, Pallas kernels for 0% -> 0%
where the time goes in v2:
time: 252 us
  Pallas kernels  110 us (44%)
  waiting for transfers between devices  72.4 us (29%)
  matrix products  30.1 us (12%)
  starting transfers between devices  22.2 us (9%)
  local copies, waits for them, and re-layouts  12.1 us (5%)
  other arithmetic  4.03 us (2%)
    pallas_call x1, Pallas kernels, attention(): pl.pallas_call(functools.partial(attention_back, blk_dev, kmax), grid_spe...  61.9 us
    pallas_call x1, Pallas kernels, finish(): pl.pallas_call(functools.partial(finish_sums, owners, heads), out_shape=[...  48.1 us
    all_to_all x1, waiting for transfers between devices, on_device(): back_v = swap(far_v)  25.1 us
    all_to_all x1, waiting for transfers between devices, on_device(): k_far = swap(keys_own[wanted])  17.2 us
    all_to_all x1, waiting for transfers between devices, on_device(): v_far = swap(values_own[wanted])  16.8 us
    dot_general x3, matrix products, dot32(): return jnp.dot(a, b, preferred_element_type=jnp.float32)  12.9 us
    dot_general x4, matrix products, term(): lax.dot_general(left, right, down, preferred_element_type=jnp.float32)  12.2 us
    all_to_all x1, waiting for transfers between devices, on_device(): back_k = swap(far_k)  11.5 us
  transfers between devices with their start and end apart: 5, of which 5 were waited for; matrix products, arithmetic and copies ran while one was open for 13% of the time, Pallas kernels for 0%

profile of v2, /device:TPU:0, one launch (start us, length us, event | category | flops | bytes accessed | tf_op | source)
XLA Modules:
  0.0 251.7 jit_solution(13100442293186774739)
XLA Ops:
  0.6 6.5 %all-to-all-start = ((s32[4,1,4]{2,1,0:T(1,128)}), s32[4,1,4]{2,1,0:T(1,128)S(1)}, u32[]{:S(2)}, u32[]{:S(2)}) async-start(s32[4,1,4]{2,1,0:T(1,128)} %bitcast.50), calls=%async_computation | async-start | bytes 4096 | tf_op jit(solution)/shard_map/all_to_all | solution.py:353
  7.1 3.6 %convolution_convert_fusion.1 = bf16[2048,256]{1,0:T(8,128)(2,1)S(1)} fusion(bf16[2048,1024]{1,0:T(8,128)(2,1)} %param.9, bf16[1024,256]{1,0:T(8,128)(2,1)} %refs_8_.1), kind=kOutput, calls=%fused_computation.3 | convolution fusion | flops 1074266112 | bytes 5767168 | tf_op jit(solution)/shard_map/dot_general | solution.py:19
  10.7 1.8 all-to-all-done
  13.9 1.6 gather_fusion
  15.4 4.3 %all-to-all-start.1 = ((bf16[16,128,256]{2,1,0:T(8,128)(2,1)}), bf16[16,128,256]{2,1,0:T(8,128)(2,1)}, u32[]{:S(2)}, u32[]{:S(2)}) async-start(bf16[16,128,256]{2,1,0:T(8,128)(2,1)} %gather_fusion), calls=%async_computation.1 | async-start | bytes 2097152 | tf_op jit(solution)/shard_map/all_to_all | solution.py:355
  19.8 4.5 %convolution_convert_fusion = bf16[2048,256]{1,0:T(8,128)(2,1)} fusion(bf16[2048,1024]{1,0:T(8,128)(2,1)} %param.9, bf16[1024,256]{1,0:T(8,128)(2,1)S(1)} %copy-done.3), kind=kOutput, calls=%fused_computation.2 | convolution fusion | flops 1074266112 | bytes 5767168 | tf_op jit(solution)/shard_map/dot_general | solution.py:19
  24.3 2.8 %gather_fusion.1 = bf16[16,128,256]{2,1,0:T(8,128)(2,1)} fusion(bf16[16,128,256]{2,1,0:T(8,128)(2,1)} %bitcast.47, s32[1024]{0:T(1024)S(1)} %pad_clamp_fusion), kind=kCustom, calls=%fused_computation.1 | custom fusion | bytes 2097216 | tf_op jit(solution)/shard_map/gather | solution.py:357
  27.1 17.2 %all-to-all-done.1.k_far_ref = bf16[16,128,256]{2,1,0:T(8,128)(2,1)} async-done(((bf16[16,128,256]{2,1,0:T(8,128)(2,1)}), bf16[16,128,256]{2,1,0:T(8,128)(2,1)}, u32[]{:S(2)}, u32[]{:S(2)}) %all-to-all-start.1) | async-done | bytes 1048608 | tf_op jit(solution)/shard_map/all_to_all | solution.py:355
  44.3 3.5 %all-to-all-start.2 = ((bf16[16,128,256]{2,1,0:T(8,128)(2,1)}), bf16[16,128,256]{2,1,0:T(8,128)(2,1)S(1)}, u32[]{:S(2)}, u32[]{:S(2)}) async-start(bf16[16,128,256]{2,1,0:T(8,128)(2,1)} %gather_fusion.1), calls=%async_computation.2 | async-start | bytes 2097152 | tf_op jit(solution)/shard_map/all_to_all | solution.py:357
  49.3 4.7 %convolution_convert_fusion.3.q_ref = bf16[2048,256]{1,0:T(8,128)(2,1)} fusion(bf16[2048,1024]{1,0:T(8,128)(2,1)} %param.9, bf16[1024,256]{1,0:T(8,128)(2,1)S(1)} %copy-done.1), kind=kOutput, calls=%fused_computation.5 | convolution fusion | flops 1074266112 | bytes 5767168 | tf_op jit(solution)/shard_map/dot_general | solution.py:19
  54.0 2.3 convolution_convert_fusion.2.g_ref
  56.3 16.8 %all-to-all-done.2.v_far_ref = bf16[16,128,256]{2,1,0:T(8,128)(2,1)S(1)} async-done(((bf16[16,128,256]{2,1,0:T(8,128)(2,1)}), bf16[16,128,256]{2,1,0:T(8,128)(2,1)S(1)}, u32[]{:S(2)}, u32[]{:S(2)}) %all-to-all-start.2) | async-done | bytes 1048608 | tf_op jit(solution)/shard_map/all_to_all | solution.py:357
  73.0 1.0 copy-done.15
  74.0 61.9 %attention_back.1 = (bf16[2048,256]{1,0:T(8,128)(2,1)}, bf16[2048,256]{1,0:T(8,128)(2,1)}, f32[16,128,256]{2,1,0:T(8,128)}, f32[16,128,256]{2,1,0:T(8,128)}, bf1...) custom-call(s32[16,8]{1,0:T(8,128)} %copy.25.pattern_ref, s32[32]{0:T(128)} %pad_convert_fusion.alive_ref, ...), custom_call_target="tpu_custom_call" | custom-call | flops 6442450944 | bytes 20971520 | tf_op jit(solution)/shard_map/attention_back/pallas_call | solution.py:148
  135.9 3.5 %all-to-all-start.4 = ((bf16[16,128,256]{2,1,0:T(8,128)(2,1)}), bf16[16,128,256]{2,1,0:T(8,128)(2,1)S(1)}, u32[]{:S(2)}, u32[]{:S(2)}) async-start(bf16[16,128,256]{2,1,0:T(8,128)(2,1)} %get-tuple-element.20), calls=%async_computation.4 | async-start | bytes 2097152 | tf_op jit(solution)/shard_map/all_to_all | solution.py:366
  139.5 25.1 %all-to-all-done.4 = bf16[16,128,256]{2,1,0:T(8,128)(2,1)S(1)} async-done(((bf16[16,128,256]{2,1,0:T(8,128)(2,1)}), bf16[16,128,256]{2,1,0:T(8,128)(2,1)S(1)}, u32[]{:S(2)}, u32[]{:S(2)}) %all-to-all-start.4) | async-done | bytes 1048608 | tf_op jit(solution)/shard_map/all_to_all | solution.py:366
  164.6 4.4 %all-to-all-start.3 = ((bf16[16,128,256]{2,1,0:T(8,128)(2,1)}), bf16[16,128,256]{2,1,0:T(8,128)(2,1)}, u32[]{:S(2)}, u32[]{:S(2)}) async-start(bf16[16,128,256]{2,1,0:T(8,128)(2,1)} %get-tuple-element.18), calls=%async_computation.3 | async-start | bytes 2097152 | tf_op jit(solution)/shard_map/all_to_all | solution.py:365
  169.1 5.2 %fusion.5.refs_3_ = bf16[1024,256]{1,0:T(8,128)(2,1)} fusion(bf16[2048,256]{1,0:T(8,128)(2,1)} %get-tuple-element.21, bf16[2048,1024]{1,0:T(8,128)(2,1)} %param.10), kind=kOutput, calls=%fused_computation.17 | convolution fusion | flops 1074003968 | bytes 5767168 | tf_op jit(solution)/shard_map/dot_general | solution.py:368
  174.3 2.6 %fusion.2.refs_0_ = bf16[1024,256]{1,0:T(8,128)(2,1)} fusion(bf16[2048,256]{1,0:T(8,128)(2,1)S(1)} %copy-done.21, bf16[2048,1024]{1,0:T(8,128)(2,1)S(1)} %copy-done.18), kind=kOutput, calls=%fused_computation.14 | convolution fusion | flops 1074003968 | bytes 5767168 | tf_op jit(solution)/shard_map/dot_general | solution.py:368
  177.0 0.7 fusion.6
  177.7 1.4 fusion
  179.1 1.0 copy-done.12
  180.1 2.6 %fusion.4.refs_2_ = bf16[1024,256]{1,0:T(8,128)(2,1)} fusion(bf16[2048,256]{1,0:T(8,128)(2,1)S(1)} %bitcast.41, bf16[2048,1024]{1,0:T(8,128)(2,1)S(1)} %copy-done.18), kind=kOutput, calls=%fused_computation.16 | convolution fusion | flops 1074003968 | bytes 5767168 | tf_op jit(solution)/shard_map/dot_general | solution.py:368
  182.7 11.5 %all-to-all-done.3 = bf16[16,128,256]{2,1,0:T(8,128)(2,1)} async-done(((bf16[16,128,256]{2,1,0:T(8,128)(2,1)}), bf16[16,128,256]{2,1,0:T(8,128)(2,1)}, u32[]{:S(2)}, u32[]{:S(2)}) %all-to-all-start.3) | async-done | bytes 1048608 | tf_op jit(solution)/shard_map/all_to_all | solution.py:365
  194.2 2.1 fusion.8
  196.3 1.3 fusion.1
  197.7 1.7 fusion.3.refs_1_
  199.7 48.1 %finish_sums.1 = (f32[256,256]{1,0:T(8,128)S(1)}, f32[256,256]{1,0:T(8,128)S(1)}, f32[256,256]{1,0:T(8,128)S(1)}, f32[256,256]{1,0:T(8,128)S(1)}, bf16[2048,256]{1,0:T(8,128)(2,1)S(1)}) custom-call(bf16[1024,256]{1,0:T(8,128)(2,1)S(1)} %copy-done.6, bf16[1024,256]{1,0:T(8,128)(2,1)S(1)} %fusion.3.refs_1_, bf16[1024,256]{1,0:T(8,128)(2,1)S(1)} %copy-done.7, ...), custom_call_target="tpu_custom_call" | custom-call | flops 3221225472 | bytes 10485760 | tf_op jit(solution)/shard_map/finish_sums/pallas_call | solution.py:313
  247.8 0.8 copy.34
  248.7 1.0 copy.53
  249.6 0.7 copy.54
  251.0 0.7 copy.56
  (53 shorter events, 3.8 us)
Async XLA Ops:
  0.6 53.4 %copy-start = (bf16[256,1024]{1,0:T(8,128)(2,1)S(1)}, bf16[256,1024]{1,0:T(8,128)(2,1)}, u32[]{:S(2)}) copy-start(bf16[256,1024]{1,0:T(8,128)(2,1)} %param.14) | copy-start | bytes 1572868
  0.6 11.9 %all-to-all-start = ((s32[4,1,4]{2,1,0:T(1,128)}), s32[4,1,4]{2,1,0:T(1,128)S(1)}, u32[]{:S(2)}, u32[]{:S(2)}) async-start(s32[4,1,4]{2,1,0:T(1,128)} %bitcast.50), calls=%async_computation | async-start | bytes 4096 | tf_op jit(solution)/shard_map/all_to_all | solution.py:353
  7.1 12.6 %copy-start.3 = (bf16[1024,256]{1,0:T(8,128)(2,1)S(1)}, bf16[1024,256]{1,0:T(8,128)(2,1)}, u32[]{:S(2)}) copy-start(bf16[1024,256]{1,0:T(8,128)(2,1)} %refs_9_.1) | copy-start | bytes 1572868
  10.7 13.6 %copy-start.14 = (bf16[2048,256]{1,0:T(8,128)(2,1)}, bf16[2048,256]{1,0:T(8,128)(2,1)S(1)}, u32[]{:S(2)}) copy-start(bf16[2048,256]{1,0:T(8,128)(2,1)S(1)} %convolution_convert_fusion.1) | copy-start | bytes 3145732
  15.4 28.9 %all-to-all-start.1 = ((bf16[16,128,256]{2,1,0:T(8,128)(2,1)}), bf16[16,128,256]{2,1,0:T(8,128)(2,1)}, u32[]{:S(2)}, u32[]{:S(2)}) async-start(bf16[16,128,256]{2,1,0:T(8,128)(2,1)} %gather_fusion), calls=%async_computation.1 | async-start | bytes 2097152 | tf_op jit(solution)/shard_map/all_to_all | solution.py:355
  19.7 28.1 %copy-start.20 = (s32[1,4]{1,0:T(1,128)S(1)}, s32[1,4]{1,0:T(1,128)}, u32[]{:S(2)}) copy-start(s32[1,4]{1,0:T(1,128)} %param.16) | copy-start | bytes 52
  19.7 28.3 %copy-start.16 = (s32[16,8]{0,1:T(8,128)S(1)}, s32[16,8]{0,1:T(8,128)}, u32[]{:S(2)}) copy-start(s32[16,8]{0,1:T(8,128)} %param.17) | copy-start | bytes 1540
  19.7 29.6 %copy-start.1 = (bf16[1024,256]{1,0:T(8,128)(2,1)S(1)}, bf16[1024,256]{1,0:T(8,128)(2,1)}, u32[]{:S(2)}) copy-start(bf16[1024,256]{1,0:T(8,128)(2,1)} %refs_7_.1) | copy-start | bytes 1572868
  44.3 28.7 %all-to-all-start.2 = ((bf16[16,128,256]{2,1,0:T(8,128)(2,1)}), bf16[16,128,256]{2,1,0:T(8,128)(2,1)S(1)}, u32[]{:S(2)}, u32[]{:S(2)}) async-start(bf16[16,128,256]{2,1,0:T(8,128)(2,1)} %gather_fusion.1), calls=%async_computation.2 | async-start | bytes 2097152 | tf_op jit(solution)/shard_map/all_to_all | solution.py:357
  48.7 5.3 %copy-start.17 = (bf16[2048,1024]{1,0:T(8,128)(2,1)S(1)}, bf16[2048,1024]{1,0:T(8,128)(2,1)}, u32[]{:S(2)}) copy-start(bf16[2048,1024]{1,0:T(8,128)(2,1)} %param.10) | copy-start | bytes 12582916
  73.0 1.0 copy-start.15
  135.9 28.7 %all-to-all-start.4 = ((bf16[16,128,256]{2,1,0:T(8,128)(2,1)}), bf16[16,128,256]{2,1,0:T(8,128)(2,1)S(1)}, u32[]{:S(2)}, u32[]{:S(2)}) async-start(bf16[16,128,256]{2,1,0:T(8,128)(2,1)} %get-tuple-element.20), calls=%async_computation.4 | async-start | bytes 2097152 | tf_op jit(solution)/shard_map/all_to_all | solution.py:366
  164.6 9.7 %copy-start.8 = (bf16[16,128,256]{2,1,0:T(8,128)(2,1)}, bf16[16,128,256]{2,1,0:T(8,128)(2,1)S(1)}, u32[]{:S(2)}) copy-start(bf16[16,128,256]{2,1,0:T(8,128)(2,1)S(1)} %all-to-all-done.4) | copy-start | bytes 3145732
  164.6 29.5 %all-to-all-start.3 = ((bf16[16,128,256]{2,1,0:T(8,128)(2,1)}), bf16[16,128,256]{2,1,0:T(8,128)(2,1)}, u32[]{:S(2)}, u32[]{:S(2)}) async-start(bf16[16,128,256]{2,1,0:T(8,128)(2,1)} %get-tuple-element.18), calls=%async_computation.3 | async-start | bytes 2097152 | tf_op jit(solution)/shard_map/all_to_all | solution.py:365
  169.1 5.2 %copy-start.18 = (bf16[2048,1024]{1,0:T(8,128)(2,1)S(1)}, bf16[2048,1024]{1,0:T(8,128)(2,1)}, u32[]{:S(2)}) copy-start(bf16[2048,1024]{1,0:T(8,128)(2,1)} %param.9) | copy-start | bytes 12582916
  169.1 5.2 %copy-start.21 = (bf16[2048,256]{1,0:T(8,128)(2,1)S(1)}, bf16[2048,256]{1,0:T(8,128)(2,1)}, u32[]{:S(2)}) copy-start(bf16[2048,256]{1,0:T(8,128)(2,1)} %get-tuple-element.16.refs_4_) | copy-start | bytes 3145732
  174.3 2.7 %copy-start.9 = (bf16[16,128,256]{2,1,0:T(8,128)(2,1)S(1)}, bf16[16,128,256]{2,1,0:T(8,128)(2,1)}, u32[]{:S(2)}) copy-start(bf16[16,128,256]{2,1,0:T(8,128)(2,1)} %copy-done.8) | copy-start | bytes 3145732
  174.3 3.4 %copy-start.11 = (f32[16,128,256]{2,1,0:T(8,128)S(1)}, f32[16,128,256]{2,1,0:T(8,128)}, u32[]{:S(2)}) copy-start(f32[16,128,256]{2,1,0:T(8,128)} %get-tuple-element.19) | copy-start | bytes 6291460
  179.1 1.0 copy-start.12
  180.1 16.2 %copy-start.10 = (f32[16,128,256]{2,1,0:T(8,128)S(1)}, f32[16,128,256]{2,1,0:T(8,128)}, u32[]{:S(2)}) copy-start(f32[16,128,256]{2,1,0:T(8,128)} %get-tuple-element.17) | copy-start | bytes 6291460
  194.2 3.5 %copy-start.19 = (bf16[2048,1024]{1,0:T(8,128)(2,1)S(1)}, bf16[2048,1024]{1,0:T(8,128)(2,1)}, u32[]{:S(2)}) copy-start(bf16[2048,1024]{1,0:T(8,128)(2,1)} %param.9) | copy-start | bytes 12582916
  197.6 1.8 copy-start.13
  197.6 1.8 copy-start.2
  197.6 1.8 copy-start.4
  197.6 1.8 copy-start.5
  197.6 1.9 copy-start.6
  197.7 2.0 copy-start.7

commit v3 on v2

--- a/solution.py
+++ b/solution.py
@@ -187,19 +187,23 @@
 
 
 def finish_sums(owners, heads, *refs):
-    terms, (gq_ref, gk_ref, gv_ref, wq_ref, wk_ref, wv_ref) = refs[:TERMS], refs[TERMS : TERMS + 6]
-    sums, dx_ref = refs[TERMS + 6 : 2 * TERMS + 6], refs[2 * TERMS + 6]
-    (x_ref, near, mixed, far, got, near_send, near_recv, far_send, far_recv, got_send, got_recv) = refs[
-        2 * TERMS + 7 :
+    (owned_ref, tokens_ref, d_out_ref, att_ref, gq_ref, own_k, own_v, far_k, far_v) = refs[:9]
+    (wq_ref, wk_ref, wv_ref), sums, dx_ref = refs[9:12], refs[12 : 12 + TERMS], refs[12 + TERMS]
+    (back, spread, gk_ref, gv_ref, terms, x_ref, near, mixed, far, got) = refs[13 + TERMS : 23 + TERMS]
+    (back_send, back_recv, near_send, near_recv, far_send, far_recv, got_send, got_recv) = refs[
+        23 + TERMS :
     ]
     chips = heads // 2
     owner = lax.axis_index("owner")
     head = lax.axis_index("head")
     chip, core = head // 2, head % 2
     partner = chip * 2 + (1 - core)
-    part = terms[0].shape[0] // owners
+    depth, width = terms.shape[1:]
+    part = depth // owners
     rows, cols = dx_ref.shape
     step = rows // CHUNKS
+    blk_dev = own_k.shape[0]
+    cap = back.shape[2]
 
     barrier = pltpu.get_barrier_semaphore()
     for off in range(1, owners):
@@ -216,12 +220,35 @@
         )
     pl.semaphore_wait(barrier, owners - 1 + 1 + chips - 1)
 
-    sends = []
-    for t in range(TERMS):
+    back_copies = []
+    for t, listed in enumerate((far_k, far_v)):
         for off in range(1, owners):
             to = lax.rem(owner + off, owners)
             copy = pltpu.make_async_remote_copy(
-                src_ref=terms[t].at[pl.ds(pl.multiple_of(to * part, part), part)],
+                src_ref=listed.at[pl.ds(to * cap, cap)],
+                dst_ref=back.at[t, off],
+                send_sem=back_send.at[t, off - 1],
+                recv_sem=back_recv.at[t, off - 1],
+                device_id={"owner": to},
+                device_id_type=MESH_ID,
+            )
+            copy.start()
+            back_copies.append(copy)
+        back[t, 0] = listed[pl.ds(owner * cap, cap)]
+
+    def make_term(t, left_ref, right_ref):
+        turned = right_ref[...].T
+        tile = min(depth, 256)
+        for n in range(0, depth, tile):
+            terms[t, n : n + tile] = dot32(turned, left_ref[:, n : n + tile]).T.astype(jnp.bfloat16)
+
+    sends = [[] for _ in range(TERMS)]
+
+    def send_term(t):
+        for off in range(1, owners):
+            to = lax.rem(owner + off, owners)
+            copy = pltpu.make_async_remote_copy(
+                src_ref=terms.at[t, pl.ds(pl.multiple_of(to * part, part), part)],
                 dst_ref=got.at[t, off - 1],
                 send_sem=got_send.at[t, off - 1],
                 recv_sem=got_recv.at[t, off - 1],
@@ -229,7 +256,36 @@
                 device_id_type=MESH_ID,
             )
             copy.start()
-            sends.append(copy)
+            sends[t].append(copy)
+
+    make_term(0, tokens_ref, gq_ref)
+    make_term(3, d_out_ref, att_ref)
+    for copy in back_copies:
+        copy.wait_recv()
+    send_term(0)
+    send_term(3)
+
+    group = math.gcd(4, blk_dev)
+    low = jnp.bfloat16
+    one = (
+        lax.broadcasted_iota(jnp.int32, (BLOCK, BLOCK), 0)
+        == lax.broadcasted_iota(jnp.int32, (BLOCK, BLOCK), 1)
+    ).astype(jnp.float32)
+    arrived_k = back[0].reshape(owners * cap * BLOCK, width)
+    arrived_v = back[1].reshape(owners * cap * BLOCK, width)
+    for e0 in range(0, blk_dev, group):
+        for e in range(group):
+            for off in range(owners):
+                source = lax.rem(owner + owners - off, owners)
+                for c in range(cap):
+                    at = (off * cap + c) * BLOCK
+                    spread[e * BLOCK : (e + 1) * BLOCK, at : at + BLOCK] = (
+                        one * owned_ref[e0 + e, source * cap + c]
+                    ).astype(low)
+        here = slice(e0 * BLOCK, (e0 + group) * BLOCK)
+        for own, arrived, grad in ((own_k, arrived_k, gk_ref), (own_v, arrived_v, gv_ref)):
+            local = own[e0 : e0 + group].reshape(group * BLOCK, width)
+            grad[here] = (local + dot32(spread[...], arrived)).astype(low)
 
     weights = jnp.concatenate([wq_ref[...], wk_ref[...], wv_ref[...]], axis=1)
     near_copies = []
@@ -256,6 +312,12 @@
             copy.start()
             copies.append(copy)
         near_copies.append(copies)
+        if c == 0:
+            make_term(1, tokens_ref, gk_ref)
+            send_term(1)
+        if c == 1:
+            make_term(2, tokens_ref, gv_ref)
+            send_term(2)
 
     far_copies = []
     for c in range(CHUNKS):
@@ -289,63 +351,68 @@
             total += far[off, here].astype(jnp.float32)
         dx_ref[here] = total.astype(jnp.bfloat16)
     for t in range(TERMS):
-        total = terms[t][pl.ds(pl.multiple_of(owner * part, part), part)].astype(jnp.float32)
+        total = terms[t, pl.ds(pl.multiple_of(owner * part, part), part)].astype(jnp.float32)
         for off in range(owners - 1):
-            sends[t * (owners - 1) + off].wait_recv()
+            sends[t][off].wait_recv()
             total += got[t, off].astype(jnp.float32)
         sums[t][...] = total
-    for copy in sends:
+    for copy in back_copies:
         copy.wait_send()
-    for copies in near_copies + far_copies:
+    for copies in sends + near_copies + far_copies:
         for copy in copies:
             copy.wait_send()
 
 
-def finish(terms, grads, weights):
+def finish(owned, tokens, d_out, attended, grad_q, own, listed, weights):
     owners = lax.axis_size("owner")
     heads = lax.axis_size("head")
     chips = heads // 2
-    depth, width = terms[0].shape
-    rows = grads[0].shape[0]
+    rows, depth = tokens.shape
+    width = grad_q.shape[1]
+    slots = listed[0].shape[0]
+    cap = slots // owners
     part, cols = depth // owners, depth // heads
+    group = math.gcd(4, own[0].shape[0])
     low = jnp.bfloat16
     vmem = pl.BlockSpec(memory_space=pltpu.VMEM)
+    pairs = lambda *shape: [pltpu.SemaphoreType.DMA(shape)] * 2
     return pl.pallas_call(
         functools.partial(finish_sums, owners, heads),
         out_shape=[jax.ShapeDtypeStruct((part, width), jnp.float32)] * TERMS
         + [jax.ShapeDtypeStruct((rows, cols), low)],
-        in_specs=[vmem] * (TERMS + 6),
+        in_specs=[pl.BlockSpec(memory_space=pltpu.SMEM)] + [vmem] * 11,
         out_specs=[vmem] * (TERMS + 1),
         scratch_shapes=[
+            pltpu.VMEM((2, owners, cap, BLOCK, width), low),
+            pltpu.VMEM((group * BLOCK, slots * BLOCK), low),
+            pltpu.VMEM((rows, width), low),
+            pltpu.VMEM((rows, width), low),
+            pltpu.VMEM((TERMS, depth, width), low),
             pltpu.VMEM((heads, rows, cols), low),
             pltpu.VMEM((chips, rows, cols), low),
             pltpu.VMEM((chips - 1, rows, cols), low),
             pltpu.VMEM((chips - 1, rows, cols), low),
             pltpu.VMEM((TERMS, owners - 1, part, width), low),
-            pltpu.SemaphoreType.DMA((CHUNKS, chips)),
-            pltpu.SemaphoreType.DMA((CHUNKS, chips)),
-            pltpu.SemaphoreType.DMA((CHUNKS, chips - 1)),
-            pltpu.SemaphoreType.DMA((CHUNKS, chips - 1)),
-            pltpu.SemaphoreType.DMA((TERMS, owners - 1)),
-            pltpu.SemaphoreType.DMA((TERMS, owners - 1)),
-        ],
+        ]
+        + pairs(2, owners - 1)
+        + pairs(CHUNKS, chips)
+        + pairs(CHUNKS, chips - 1)
+        + pairs(TERMS, owners - 1),
         compiler_params=pltpu.CompilerParams(
-            collective_id=0, has_side_effects=True, vmem_limit_bytes=48 * 2**20
+            collective_id=0, has_side_effects=True, vmem_limit_bytes=56 * 2**20
         ),
         cost_estimate=pl.CostEstimate(
-            flops=6 * rows * depth * width, bytes_accessed=10 * 2**20, transcendentals=0
+            flops=16 * rows * depth * width, bytes_accessed=20 * 2**20, transcendentals=0
         ),
         name="finish_sums",
-    )(*terms, *grads, *weights)
+    )(owned, tokens, d_out, attended, grad_q, *own, *listed, *weights)
 
 
 def on_device(tokens, d_out, w_query, w_key, w_value, w_out, fetch_list, fetch_count, pattern):
     blk_dev, kmax = pattern.shape
     cap = fetch_list.shape[2]
     width = w_query.shape[1]
-    rows = tokens.shape[0]
     across = (((1,), (1,)), ((), ()))
-    down = (((0,), (0,)), ((), ()))
     low = jnp.bfloat16
     swap = functools.partial(
         lax.all_to_all, axis_name="owner", split_axis=0, concat_axis=0, tiled=True
@@ -362,24 +429,16 @@
     attended, grad_q, own_k, own_v, far_k, far_v = attention(
         pattern, alive, query, grad_attn, keys_own, values_own, k_far, v_far
     )
-    back_k = swap(far_k)
-    back_v = swap(far_v)
-    def term(left, right):
-        return lax.dot_general(left, right, down, preferred_element_type=jnp.float32).astype(low)
-
-    term_o = term(d_out, attended)
-    term_q = term(tokens, grad_q)
-    owned = (jnp.arange(blk_dev, dtype=jnp.int32)[:, None] == wanted[None, :]).astype(low)
-
-    def collect(own, back):
-        far = jnp.einsum("ek,kbd->ebd", owned, back, preferred_element_type=jnp.float32)
-        return (own + far).astype(low).reshape(rows, width)
-
-    grad_k = collect(own_k, back_k)
-    grad_v = collect(own_v, back_v)
-    terms = (term_q, term(tokens, grad_k), term(tokens, grad_v), term_o)
+    owned = jnp.arange(blk_dev, dtype=jnp.int32)[:, None] == wanted[None, :]
     sum_q, sum_k, sum_v, sum_o, d_tokens = finish(
-        terms, (grad_q, grad_k, grad_v), (w_query, w_key, w_value)
+        owned.astype(jnp.float32),
+        tokens,
+        d_out,
+        attended,
+        grad_q,
+        (own_k, own_v),
+        (far_k, far_v),
+        (w_query, w_key, w_value),
     )
     return (d_tokens, sum_q, sum_k, sum_v, sum_o.T)
 

time: 252 us -> 244 us (0.968)
  Pallas kernels: 110 us -> 161 us
  waiting for transfers between devices: 72.4 us -> 36.1 us
  matrix products: 30.1 us -> 14.2 us
  starting transfers between devices: 22.2 us -> 14.2 us
  local copies, waits for them, and re-layouts: 12.1 us -> 14.8 us
    pallas_call x1, Pallas kernels: 48.1 us -> 99.2 us  [finish(): pl.pallas_call(functools.partial(finish_sums, owners, heads), out_shape=[...]
    all_to_all x2 -> x0, waiting for transfers between devices: 36.6 us -> none  [the longest x1 25.1 us: on_device(): back_v = swap(far_v)]
    dot_general x6 -> x0, matrix products: 15 us -> none  [the longest x4 12.2 us: term(): lax.dot_general(left, right, down, preferred_element_type=jnp.float32)]
    all_to_all x2 -> x0, starting transfers between devices: 7.97 us -> none  [the longest x1 4.44 us: on_device(): back_k = swap(far_k)]
    unnamed x50 -> x22, local copies, waits for them, and re-layouts: 6.87 us -> 10.8 us
  transfers between devices with their start and end apart: 5 -> 3, of which waited for: 5 -> 3; matrix products, arithmetic and copies ran while one was open for 13% -> 8% of each run, Pallas kernels for 0% -> 0%
where the time goes in v3:
time: 244 us; the launch traced here: 243 us
  Pallas kernels  161 us (66%)
  waiting for transfers between devices  36.1 us (15%)
  local copies, waits for them, and re-layouts  14.8 us (6%)
  starting transfers between devices  14.2 us (6%)
  matrix products  14.2 us (6%)
    pallas_call x1, Pallas kernels, finish(): pl.pallas_call(functools.partial(finish_sums, owners, heads), out_shape=[...  99.2 us
    pallas_call x1, Pallas kernels, attention(): pl.pallas_call(functools.partial(attention_back, blk_dev, kmax), grid_spe...  61.8 us
    all_to_all x1, waiting for transfers between devices, on_device(): k_far = swap(keys_own[wanted])  19.4 us
    all_to_all x1, waiting for transfers between devices, on_device(): v_far = swap(values_own[wanted])  14.8 us
    dot_general x3, matrix products, dot32(): return jnp.dot(a, b, preferred_element_type=jnp.float32)  11.9 us
    unnamed x22, local copies, waits for them, and re-layouts  10.8 us
    all_to_all x1, starting transfers between devices, on_device(): wanted = swap(fetch_list[0]).reshape(-1)  6.46 us
  transfers between devices with their start and end apart: 3, of which 3 were waited for; matrix products, arithmetic and copies ran while one was open for 8% of the time, Pallas kernels for 0%

profile of v3, /device:TPU:0, one launch (start us, length us, event | category | flops | bytes accessed | tf_op | source)
XLA Modules:
  0.0 243.0 jit_solution(14357717097711339)
XLA Ops:
  0.6 0.0 copy-start
  0.6 6.5 %all-to-all-start = ((s32[4,1,4]{2,1,0:T(1,128)}), s32[4,1,4]{2,1,0:T(1,128)S(1)}, u32[]{:S(2)}, u32[]{:S(2)}) async-start(s32[4,1,4]{2,1,0:T(1,128)} %bitcast.24), calls=%async_computation | async-start | bytes 4096 | tf_op jit(solution)/shard_map/all_to_all | solution.py:420
  7.1 3.6 %convolution_convert_fusion.1 = bf16[2048,256]{1,0:T(8,128)(2,1)S(1)} fusion(bf16[2048,1024]{1,0:T(8,128)(2,1)} %refs_1_.1, bf16[1024,256]{1,0:T(8,128)(2,1)} %refs_10_.1), kind=kOutput, calls=%fused_computation.3 | convolution fusion | flops 1074266112 | bytes 5767168 | tf_op jit(solution)/shard_map/dot_general | solution.py:19
  10.7 1.9 all-to-all-done
  12.6 0.1 reshape.62
  12.7 1.6 gather_fusion
  14.3 4.3 %all-to-all-start.1 = ((bf16[16,128,256]{2,1,0:T(8,128)(2,1)}), bf16[16,128,256]{2,1,0:T(8,128)(2,1)}, u32[]{:S(2)}, u32[]{:S(2)}) async-start(bf16[16,128,256]{2,1,0:T(8,128)(2,1)} %gather_fusion), calls=%async_computation.1 | async-start | bytes 2097152 | tf_op jit(solution)/shard_map/all_to_all | solution.py:422
  18.5 0.0 copy-start.4
  18.6 0.0 copy-start.6
  18.6 3.6 %convolution_convert_fusion = bf16[2048,256]{1,0:T(8,128)(2,1)S(1)} fusion(bf16[2048,1024]{1,0:T(8,128)(2,1)} %refs_1_.1, bf16[1024,256]{1,0:T(8,128)(2,1)} %refs_11_.1), kind=kOutput, calls=%fused_computation.2 | convolution fusion | flops 1074266112 | bytes 5767168 | tf_op jit(solution)/shard_map/dot_general | solution.py:19
  22.2 1.6 gather_fusion.1
  23.8 19.4 %all-to-all-done.1.k_far_ref = bf16[16,128,256]{2,1,0:T(8,128)(2,1)} async-done(((bf16[16,128,256]{2,1,0:T(8,128)(2,1)}), bf16[16,128,256]{2,1,0:T(8,128)(2,1)}, u32[]{:S(2)}, u32[]{:S(2)}) %all-to-all-start.1) | async-done | bytes 1048608 | tf_op jit(solution)/shard_map/all_to_all | solution.py:422
  43.2 3.5 %all-to-all-start.2 = ((bf16[16,128,256]{2,1,0:T(8,128)(2,1)}), bf16[16,128,256]{2,1,0:T(8,128)(2,1)S(1)}, u32[]{:S(2)}, u32[]{:S(2)}) async-start(bf16[16,128,256]{2,1,0:T(8,128)(2,1)} %gather_fusion.1), calls=%async_computation.2 | async-start | bytes 2097152 | tf_op jit(solution)/shard_map/all_to_all | solution.py:424
  46.7 0.7 copy.17.pattern_ref
  47.4 0.1 iota_compare_fusion.1
  47.5 0.1 convert_element_type.20
  47.5 0.6 pad_convert_fusion.alive_ref
  48.1 4.7 %convolution_convert_fusion.3.q_ref = bf16[2048,256]{1,0:T(8,128)(2,1)} fusion(bf16[2048,1024]{1,0:T(8,128)(2,1)} %refs_1_.1, bf16[1024,256]{1,0:T(8,128)(2,1)S(1)} %copy-done.6), kind=kOutput, calls=%fused_computation.5 | convolution fusion | flops 1074266112 | bytes 5767168 | tf_op jit(solution)/shard_map/dot_general | solution.py:19
  52.9 2.3 convolution_convert_fusion.2.g_ref
  55.2 0.5 broadcast.40
  55.7 0.7 reduce.5
  56.3 0.1 eq.16
  56.4 0.6 fusion.refs_0_
  57.0 14.8 %all-to-all-done.2.v_far_ref = bf16[16,128,256]{2,1,0:T(8,128)(2,1)S(1)} async-done(((bf16[16,128,256]{2,1,0:T(8,128)(2,1)}), bf16[16,128,256]{2,1,0:T(8,128)(2,1)S(1)}, u32[]{:S(2)}, u32[]{:S(2)}) %all-to-all-start.2) | async-done | bytes 1048608 | tf_op jit(solution)/shard_map/all_to_all | solution.py:424
  71.9 1.1 copy-done.3
  72.9 61.8 %attention_back.1 = (bf16[2048,256]{1,0:T(8,128)(2,1)}, bf16[2048,256]{1,0:T(8,128)(2,1)}, f32[16,128,256]{2,1,0:T(8,128)}, f32[16,128,256]{2,1,0:T(8,128)}, bf1...) custom-call(s32[16,8]{1,0:T(8,128)} %copy.17.pattern_ref, s32[32]{0:T(128)} %pad_convert_fusion.alive_ref, ...), custom_call_target="tpu_custom_call" | custom-call | flops 6442450944 | bytes 20971520 | tf_op jit(solution)/shard_map/attention_back/pallas_call | solution.py:148
  134.8 99.2 %finish_sums.1 = (f32[256,256]{1,0:T(8,128)}, f32[256,256]{1,0:T(8,128)}, f32[256,256]{1,0:T(8,128)}, f32[256,256]{1,0:T(8,128)}, bf16[2048,256]{1,0:T(8,128)(2,1)}) custom-call(f32[16,16]{1,0:T(8,128)} %fusion.refs_0_, bf16[2048,1024]{1,0:T(8,128)(2,1)} %refs_1_.1, bf16[2048,1024]{1,0:T(8,128)(2,1)} %refs_2_.1, ...), custom_call_target="tpu_custom_call" | custom-call | flops 8589934592 | bytes 20971520 | tf_op jit(solution)/shard_map/finish_sums/pallas_call | solution.py:379
  234.0 1.8 copy.18
  235.7 2.3 copy.23
  238.0 1.7 copy.24
  239.7 1.7 copy.25
  241.3 1.7 copy.26
  (14 shorter events, 0.0 us)
Async XLA Ops:
  0.6 52.2 %copy-start = (bf16[256,1024]{1,0:T(8,128)(2,1)S(1)}, bf16[256,1024]{1,0:T(8,128)(2,1)}, u32[]{:S(2)}) copy-start(bf16[256,1024]{1,0:T(8,128)(2,1)} %param.14) | copy-start | bytes 1572868
  0.6 11.9 %all-to-all-start = ((s32[4,1,4]{2,1,0:T(1,128)}), s32[4,1,4]{2,1,0:T(1,128)S(1)}, u32[]{:S(2)}, u32[]{:S(2)}) async-start(s32[4,1,4]{2,1,0:T(1,128)} %bitcast.24), calls=%async_computation | async-start | bytes 4096 | tf_op jit(solution)/shard_map/all_to_all | solution.py:420
  10.7 11.5 %copy-start.1 = (bf16[2048,256]{1,0:T(8,128)(2,1)}, bf16[2048,256]{1,0:T(8,128)(2,1)S(1)}, u32[]{:S(2)}) copy-start(bf16[2048,256]{1,0:T(8,128)(2,1)S(1)} %convolution_convert_fusion.1) | copy-start | bytes 3145732
  14.3 28.9 %all-to-all-start.1 = ((bf16[16,128,256]{2,1,0:T(8,128)(2,1)}), bf16[16,128,256]{2,1,0:T(8,128)(2,1)}, u32[]{:S(2)}, u32[]{:S(2)}) async-start(bf16[16,128,256]{2,1,0:T(8,128)(2,1)} %gather_fusion), calls=%async_computation.1 | async-start | bytes 2097152 | tf_op jit(solution)/shard_map/all_to_all | solution.py:422
  18.5 28.2 %copy-start.4 = (s32[16,8]{0,1:T(8,128)S(1)}, s32[16,8]{0,1:T(8,128)}, u32[]{:S(2)}) copy-start(s32[16,8]{0,1:T(8,128)} %param.17) | copy-start | bytes 1540
  18.6 28.8 %copy-start.7 = (s32[1,4]{1,0:T(1,128)S(1)}, s32[1,4]{1,0:T(1,128)}, u32[]{:S(2)}) copy-start(s32[1,4]{1,0:T(1,128)} %param.16) | copy-start | bytes 52
  18.6 29.6 %copy-start.6 = (bf16[1024,256]{1,0:T(8,128)(2,1)S(1)}, bf16[1024,256]{1,0:T(8,128)(2,1)}, u32[]{:S(2)}) copy-start(bf16[1024,256]{1,0:T(8,128)(2,1)} %refs_9_.1) | copy-start | bytes 1572868
  22.2 30.6 %copy-start.2 = (bf16[2048,256]{1,0:T(8,128)(2,1)}, bf16[2048,256]{1,0:T(8,128)(2,1)S(1)}, u32[]{:S(2)}) copy-start(bf16[2048,256]{1,0:T(8,128)(2,1)S(1)} %convolution_convert_fusion) | copy-start | bytes 3145732
  43.2 28.7 %all-to-all-start.2 = ((bf16[16,128,256]{2,1,0:T(8,128)(2,1)}), bf16[16,128,256]{2,1,0:T(8,128)(2,1)S(1)}, u32[]{:S(2)}, u32[]{:S(2)}) async-start(bf16[16,128,256]{2,1,0:T(8,128)(2,1)} %gather_fusion.1), calls=%async_computation.2 | async-start | bytes 2097152 | tf_op jit(solution)/shard_map/all_to_all | solution.py:424
  47.5 5.3 %copy-start.5 = (bf16[2048,1024]{1,0:T(8,128)(2,1)S(1)}, bf16[2048,1024]{1,0:T(8,128)(2,1)}, u32[]{:S(2)}) copy-start(bf16[2048,1024]{1,0:T(8,128)(2,1)} %refs_2_.1) | copy-start | bytes 12582916
  71.9 1.1 copy-start.3

commit v4 on v3

--- a/solution.py
+++ b/solution.py
@@ -49,10 +49,8 @@
     alive_ref,
     q_ref,
     g_ref,
-    k_own_ref,
-    v_own_ref,
-    k_far_ref,
-    v_far_ref,
+    own_ref,
+    far_ref,
     att_ref,
     gq_ref,
     ok_ref,
@@ -71,10 +69,10 @@
 
     @pl.when(b == 0)
     def _():
-        k_ws[:blk_dev] = k_own_ref[...]
-        v_ws[:blk_dev] = v_own_ref[...]
-        k_ws[blk_dev:] = k_far_ref[...]
-        v_ws[blk_dev:] = v_far_ref[...]
+        k_ws[:blk_dev] = own_ref[:, :, :width]
+        v_ws[:blk_dev] = own_ref[:, :, width:]
+        k_ws[blk_dev:] = far_ref[:, :, :width]
+        v_ws[blk_dev:] = far_ref[:, :, width:]
 
         def turn(e, carry):
             kt_ws[e] = k_ws[e].T
@@ -136,13 +134,14 @@
         fv_ref[...] = acc_v[blk_dev:].astype(jnp.bfloat16)
 
 
-def attention(pattern, alive, query, grad_attn, k_own, v_own, k_far, v_far):
+def attention(pattern, alive, query, grad_attn, own, far):
     blk_dev, kmax = pattern.shape
     width = query.shape[1]
-    slots = k_far.shape[0]
+    slots = far.shape[0]
     wset = blk_dev + slots
     rows = pl.BlockSpec((BLOCK, width), lambda b, *_: (b, 0))
     whole = lambda n: pl.BlockSpec((n, BLOCK, width), lambda b, *_: (0, 0, 0))
+    both = lambda n: pl.BlockSpec((n, BLOCK, 2 * width), lambda b, *_: (0, 0, 0))
     low = jnp.bfloat16
     full = jnp.float32
     return pl.pallas_call(
@@ -150,7 +149,7 @@
         grid_spec=pltpu.PrefetchScalarGridSpec(
             num_scalar_prefetch=2,
             grid=(blk_dev,),
-            in_specs=[rows, rows, whole(blk_dev), whole(blk_dev), whole(slots), whole(slots)],
+            in_specs=[rows, rows, both(blk_dev), both(slots)],
             out_specs=[rows, rows, whole(blk_dev), whole(blk_dev), whole(slots), whole(slots)],
             scratch_shapes=[
                 pltpu.VMEM((wset, BLOCK, width), low),
@@ -178,7 +177,7 @@
             transcendentals=blk_dev * BLOCK * kmax * BLOCK * (width // HEAD_DIM),
         ),
         name="attention_back",
-    )(pattern, alive, query, grad_attn, k_own, v_own, k_far, v_far)
+    )(pattern, alive, query, grad_attn, own, far)
 
 
 CHUNKS = 4
@@ -418,16 +417,15 @@
         lax.all_to_all, axis_name="owner", split_axis=0, concat_axis=0, tiled=True
     )
     wanted = swap(fetch_list[0]).reshape(-1)
-    keys_own = dot32(tokens, w_key).astype(low).reshape(blk_dev, BLOCK, width)
-    k_far = swap(keys_own[wanted])
-    values_own = dot32(tokens, w_value).astype(low).reshape(blk_dev, BLOCK, width)
-    v_far = swap(values_own[wanted])
+    pair = dot32(tokens, jnp.concatenate([w_key, w_value], axis=1)).astype(low)
+    pair = pair.reshape(blk_dev, BLOCK, 2 * width)
+    pair_far = swap(pair[wanted])
     query = dot32(tokens, w_query).astype(low)
     grad_attn = lax.dot_general(d_out, w_out, across, preferred_element_type=jnp.float32).astype(low)
     live = (jnp.arange(cap, dtype=jnp.int32)[None, :] < fetch_count[0][:, None]).reshape(-1)
     alive = jnp.concatenate([jnp.ones((blk_dev,), jnp.int32), live.astype(jnp.int32)])
     attended, grad_q, own_k, own_v, far_k, far_v = attention(
-        pattern, alive, query, grad_attn, keys_own, values_own, k_far, v_far
+        pattern, alive, query, grad_attn, pair, pair_far
     )
     owned = jnp.arange(blk_dev, dtype=jnp.int32)[:, None] == wanted[None, :]
     sum_q, sum_k, sum_v, sum_o, d_tokens = finish(

time: 244 us -> 240 us (0.984)
  starting transfers between devices: 14.2 us -> 11.7 us
    all_to_all x2 -> x1, waiting for transfers between devices: 34.2 us -> 37.4 us  [on_device(): pair_far = swap(pair[wanted])]
    convert_element_type x0 -> x1, local copies, waits for them, and re-layouts: none -> 2.86 us  [on_device(): pair = dot32(tokens, jnp.concatenate([w_key, w_value], axis=1)).astype(low)]
    all_to_all x2 -> x1, starting transfers between devices: 7.79 us -> 5.23 us  [on_device(): pair_far = swap(pair[wanted])]
    unnamed x22 -> x26, local copies, waits for them, and re-layouts: 10.8 us -> 8.28 us
    dot_general x3 -> x2, matrix products: 11.9 us -> 10.8 us  [dot32(): return jnp.dot(a, b, preferred_element_type=jnp.float32)]
  transfers between devices with their start and end apart: 3 -> 2, of which waited for: 3 -> 1; matrix products, arithmetic and copies ran while one was open for 8% -> 8% of each run, Pallas kernels for 0% -> 0%
where the time goes in v4:
time: 240 us
  Pallas kernels  161 us (67%)
  waiting for transfers between devices  37.4 us (16%)
  local copies, waits for them, and re-layouts  13.9 us (6%)
  matrix products  13.2 us (6%)
  starting transfers between devices  11.7 us (5%)
    pallas_call x1, Pallas kernels, finish(): pl.pallas_call(functools.partial(finish_sums, owners, heads), out_shape=[...  99.1 us
    pallas_call x1, Pallas kernels, attention(): pl.pallas_call(functools.partial(attention_back, blk_dev, kmax), grid_spe...  61.8 us
    all_to_all x1, waiting for transfers between devices, on_device(): pair_far = swap(pair[wanted])  37.4 us
    dot_general x2, matrix products, dot32(): return jnp.dot(a, b, preferred_element_type=jnp.float32)  10.8 us
    unnamed x26, local copies, waits for them, and re-layouts  8.28 us
    all_to_all x1, starting transfers between devices, on_device(): wanted = swap(fetch_list[0]).reshape(-1)  6.46 us
    all_to_all x1, starting transfers between devices, on_device(): pair_far = swap(pair[wanted])  5.23 us
  transfers between devices with their start and end apart: 2, of which 1 were waited for; matrix products, arithmetic and copies ran while one was open for 8% of the time, Pallas kernels for 0%

profile of v4, /device:TPU:0, one launch (start us, length us, event | category | flops | bytes accessed | tf_op | source)
XLA Modules:
  0.0 239.8 jit_solution(18003417223700275946)
XLA Ops:
  0.6 0.0 copy-start
  0.6 6.5 %all-to-all-start = ((s32[4,1,4]{2,1,0:T(1,128)}), s32[4,1,4]{2,1,0:T(1,128)S(1)}, u32[]{:S(2)}, u32[]{:S(2)}) async-start(s32[4,1,4]{2,1,0:T(1,128)} %bitcast.20), calls=%async_computation | async-start | bytes 4096 | tf_op jit(solution)/shard_map/all_to_all | solution.py:419
  7.1 6.2 %fusion = bf16[2048,512]{0,1:T(8,128)(2,1)} fusion(bf16[2048,1024]{1,0:T(8,128)(2,1)} %refs_1_.1, bf16[1024,256]{1,0:T(8,128)(2,1)} %refs_11_.1, bf16[1024,256]{1,0:T(8,128)(2,1)} %refs_10_.1), kind=kOutput, calls=%fused_computation.2 | convolution fusion | flops 2150629376 | bytes 7340032 | tf_op jit(solution)/shard_map/dot_general | solution.py:19
  13.3 2.9 %copy.18 = bf16[2048,512]{1,0:T(8,128)(2,1)S(1)} copy(bf16[2048,512]{0,1:T(8,128)(2,1)} %fusion) | data formatting | bytes 4194304 | tf_op jit(solution)/shard_map/convert_element_type | solution.py:420
  16.2 0.0 copy-start.1
  16.2 0.0 all-to-all-done
  16.2 0.1 reshape.58
  16.3 2.0 gather_fusion
  18.3 0.0 copy-done.1
  18.3 5.2 %all-to-all-start.1 = ((bf16[16,128,512]{2,1,0:T(8,128)(2,1)}), bf16[16,128,512]{2,1,0:T(8,128)(2,1)S(1)}, u32[]{:S(2)}, u32[]{:S(2)}) async-start(bf16[16,128,512]{2,1,0:T(8,128)(2,1)} %gather_fusion), calls=%async_computation.1 | async-start | bytes 4194304 | tf_op jit(solution)/shard_map/all_to_all | solution.py:422
  23.6 0.0 copy-done.6
  23.6 0.7 copy.19.pattern_ref
  24.3 0.1 iota_compare_fusion.1
  24.3 0.1 convert_element_type.20
  24.4 0.6 pad_convert_fusion.alive_ref
  25.0 4.6 %convolution_convert_fusion.2.q_ref = bf16[2048,256]{1,0:T(8,128)(2,1)} fusion(bf16[2048,1024]{1,0:T(8,128)(2,1)} %refs_1_.1, bf16[1024,256]{1,0:T(8,128)(2,1)S(1)} %copy-done.8), kind=kOutput, calls=%fused_computation.4 | convolution fusion | flops 1074266112 | bytes 5767168 | tf_op jit(solution)/shard_map/dot_general | solution.py:19
  29.6 2.4 convolution_convert_fusion.1.g_ref
  31.9 0.5 broadcast.38
  32.5 0.7 reduce.5
  33.1 0.1 eq.16
  33.2 0.6 fusion.4.refs_0_
  33.8 37.4 %all-to-all-done.1.far_ref = bf16[16,128,512]{2,1,0:T(8,128)(2,1)S(1)} async-done(((bf16[16,128,512]{2,1,0:T(8,128)(2,1)}), bf16[16,128,512]{2,1,0:T(8,128)(2,1)S(1)}, u32[]{:S(2)}, u32[]{:S(2)}) %all-to-all-start.1) | async-done | bytes 2097184 | tf_op jit(solution)/shard_map/all_to_all | solution.py:422
  71.2 1.3 copy-done.2
  72.6 61.8 %attention_back.1 = (bf16[2048,256]{1,0:T(8,128)(2,1)}, bf16[2048,256]{1,0:T(8,128)(2,1)}, f32[16,128,256]{2,1,0:T(8,128)}, f32[16,128,256]{2,1,0:T(8,128)}, bf1...) custom-call(s32[16,8]{1,0:T(8,128)} %copy.19.pattern_ref, s32[32]{0:T(128)} %pad_convert_fusion.alive_ref, ...), custom_call_target="tpu_custom_call" | custom-call | flops 6442450944 | bytes 20971520 | tf_op jit(solution)/shard_map/attention_back/pallas_call | solution.py:147
  134.4 99.1 %finish_sums.1 = (f32[256,256]{1,0:T(8,128)}, f32[256,256]{1,0:T(8,128)}, f32[256,256]{1,0:T(8,128)}, f32[256,256]{1,0:T(8,128)}, bf16[2048,256]{1,0:T(8,128)(2,1)}) custom-call(f32[16,16]{1,0:T(8,128)} %fusion.4.refs_0_, bf16[2048,1024]{1,0:T(8,128)(2,1)} %refs_1_.1, bf16[2048,1024]{1,0:T(8,128)(2,1)} %refs_2_.1, ...), custom_call_target="tpu_custom_call" | custom-call | flops 8589934592 | bytes 20971520 | tf_op jit(solution)/shard_map/finish_sums/pallas_call | solution.py:378
  233.6 1.9 copy.20
  235.4 2.3 copy.25
  237.7 0.0 copy-done.5
  237.7 0.7 copy.26
  238.4 0.7 copy.27
  239.1 0.0 copy-done.3
  239.1 0.7 copy.28
  (15 shorter events, 0.0 us)
Async XLA Ops:
  0.6 29.0 %copy-start = (bf16[256,1024]{1,0:T(8,128)(2,1)S(1)}, bf16[256,1024]{1,0:T(8,128)(2,1)}, u32[]{:S(2)}) copy-start(bf16[256,1024]{1,0:T(8,128)(2,1)} %param.14) | copy-start | bytes 1572868
  0.6 15.6 %all-to-all-start = ((s32[4,1,4]{2,1,0:T(1,128)}), s32[4,1,4]{2,1,0:T(1,128)S(1)}, u32[]{:S(2)}, u32[]{:S(2)}) async-start(s32[4,1,4]{2,1,0:T(1,128)} %bitcast.20), calls=%async_computation | async-start | bytes 4096 | tf_op jit(solution)/shard_map/all_to_all | solution.py:419
  16.2 2.1 copy-start.1
  18.3 5.2 %copy-start.6 = (s32[16,8]{0,1:T(8,128)S(1)}, s32[16,8]{0,1:T(8,128)}, u32[]{:S(2)}) copy-start(s32[16,8]{0,1:T(8,128)} %param.17) | copy-start | bytes 1540
  18.3 5.9 %copy-start.9 = (s32[1,4]{1,0:T(1,128)S(1)}, s32[1,4]{1,0:T(1,128)}, u32[]{:S(2)}) copy-start(s32[1,4]{1,0:T(1,128)} %param.16) | copy-start | bytes 52
  18.3 6.7 %copy-start.8 = (bf16[1024,256]{1,0:T(8,128)(2,1)S(1)}, bf16[1024,256]{1,0:T(8,128)(2,1)}, u32[]{:S(2)}) copy-start(bf16[1024,256]{1,0:T(8,128)(2,1)} %refs_9_.1) | copy-start | bytes 1572868
  18.3 52.9 %all-to-all-start.1 = ((bf16[16,128,512]{2,1,0:T(8,128)(2,1)}), bf16[16,128,512]{2,1,0:T(8,128)(2,1)S(1)}, u32[]{:S(2)}, u32[]{:S(2)}) async-start(bf16[16,128,512]{2,1,0:T(8,128)(2,1)} %gather_fusion), calls=%async_computation.1 | async-start | bytes 4194304 | tf_op jit(solution)/shard_map/all_to_all | solution.py:422
  25.0 4.6 %copy-start.7 = (bf16[2048,1024]{1,0:T(8,128)(2,1)S(1)}, bf16[2048,1024]{1,0:T(8,128)(2,1)}, u32[]{:S(2)}) copy-start(bf16[2048,1024]{1,0:T(8,128)(2,1)} %refs_2_.1) | copy-start | bytes 12582916
  71.2 1.3 copy-start.2
  233.5 4.1 %copy-start.5 = (f32[256,256]{1,0:T(8,128)S(1)}, f32[256,256]{1,0:T(8,128)}, u32[]{:S(2)}) copy-start(f32[256,256]{1,0:T(8,128)} %get-tuple-element.43) | copy-start | bytes 786436
  233.5 4.8 %copy-start.4 = (f32[256,256]{1,0:T(8,128)S(1)}, f32[256,256]{1,0:T(8,128)}, u32[]{:S(2)}) copy-start(f32[256,256]{1,0:T(8,128)} %get-tuple-element.44) | copy-start | bytes 786436
  233.5 5.5 %copy-start.3 = (f32[256,256]{1,0:T(8,128)S(1)}, f32[256,256]{1,0:T(8,128)}, u32[]{:S(2)}) copy-start(f32[256,256]{1,0:T(8,128)} %get-tuple-element.45) | copy-start | bytes 786436
